TPU v7x, 32 devices: a whole 2x2x4 slice. The times are simulated.
32 devices in a mesh: narrow: 2 (over y), wide: 16 (over z, x, core).
Axes of the slice: x: 2, y: 2, z: 4, core: 2. Of those that a mesh axis runs over, the one named last changes fastest.
Arguments:
- tokens: bfloat16 [65536, 384], P(('narrow', 'wide')), may hold values from -6 to 6
- cotangent: bfloat16 [65536, 384], P(('narrow', 'wide')), may hold values from -6 to 6
- valid: int32 [64, 1024], P(('narrow', 'wide')), may hold values from 0 to 1, as said below
- task_ids: int32 [64], P(('narrow', 'wide')), may hold values from 0 to 1
- top_counts: int32 [2], replicated, may hold values from 1 to 4
- expert_ids: int32 [65536, 4], P(('narrow', 'wide')), may hold values from 0 to 7, all different within a row
- attn_gain: bfloat16 [384], P('wide'), may hold values from 0.099609375 to 1.8984375
- attn_shift: bfloat16 [384], P('wide'), may hold values from -1.5 to 1.5
- proj_in: bfloat16 [384, 1152], P('wide'), may hold values from -0.3125 to 0.3125
- proj_out: bfloat16 [384, 384], P('wide'), may hold values from -4 to 4
- moe_gain: bfloat16 [384], P('wide'), may hold values from 0.099609375 to 1.8984375
- moe_shift: bfloat16 [384], P('wide'), may hold values from -1.5 to 1.5
- router: bfloat16 [2, 384, 8], P(None, 'wide'), may hold values from -0.15625 to 0.15625
- expert_in: bfloat16 [8, 384, 1536], P(None, 'wide'), may hold values from -0.3125 to 0.3125
- expert_out: bfloat16 [8, 1536, 384], P(None, 'wide'), may hold values from -1.25 to 1.25
Outputs:
- output: bfloat16 [65536, 384], P(('narrow', 'wide'))
- grad_tokens: bfloat16 [65536, 384], P(('narrow', 'wide'))
- grad_attn_gain: float32 [384], P('wide')
- grad_attn_shift: float32 [384], P('wide')
- grad_proj_in: float32 [384, 1152], P('wide')
- grad_proj_out: float32 [384, 384], P('wide')
- grad_moe_gain: float32 [384], P('wide')
- grad_moe_shift: float32 [384], P('wide')
- grad_router: float32 [2, 384, 8], P(None, 'wide')
- grad_expert_in: float32 [8, 384, 1536], P(None, 'wide')
- grad_expert_out: float32 [8, 1536, 384], P(None, 'wide')
Inputs may be any that keep to these rules, and one draw needn't show every extreme that they name: `valid`: 1 marks a patch of the image's crop, a top-left rectangle of its square grid of 1024 patches; every image has at least one patch. `expert_ids`: each row names 4 different experts.
All inputs are finite; a program needn't handle non-finite values.
Results may differ from a plain program's by a relative error of at most 0.012.
Values may be sent and summed in bfloat16 or wider, within the bound.
A program may use at most 320 MiB of HBM per device.

v0:
```python
import math

import jax
import jax.numpy as jnp
from jax import lax
from jax.sharding import PartitionSpec as P

D = 384
HEADS = 6
HEAD_DIM = 64
EXPERTS = 8
TOPMAX = 4
TASKS = 2
GRID = 1024
MICRO = 2
CAP = 256


NEGATIVE = -1e30
EPSILON = 1e-06


def normalize(values, gain, shift):
    center = values - jnp.mean(values, axis=-1, keepdims=True)
    inverse = lax.rsqrt(jnp.mean(center * center, axis=-1, keepdims=True) + EPSILON)
    unit_rows = center * inverse
    return (unit_rows * gain.astype(jnp.float32) + shift.astype(jnp.float32), unit_rows, inverse)


def normalize_back(upstream, unit_rows, inverse, gain):
    scaled = upstream * gain.astype(jnp.float32)
    centered = scaled - jnp.mean(scaled, axis=-1, keepdims=True)
    centered = centered - unit_rows * jnp.mean(scaled * unit_rows, axis=-1, keepdims=True)
    return (inverse * centered, jnp.sum(upstream * unit_rows, axis=0), jnp.sum(upstream, axis=0))


def route(valid, task_ids, top_counts, expert_ids):
    row_count = expert_ids.shape[0]
    task_match = task_ids[:, None] == jnp.arange(TASKS, dtype=jnp.int32)[None, :]
    choose = jnp.sum(jnp.where(task_match, top_counts[None, :], 0), axis=1, dtype=jnp.int32)
    per_row = jnp.repeat(choose, GRID)
    live_rows = valid.reshape(row_count) > 0
    choice_ranks = jnp.arange(TOPMAX, dtype=jnp.int32)
    used_mask = live_rows[:, None] & (choice_ranks[None, :] < per_row[:, None])
    expert_match = expert_ids[:, :, None] == jnp.arange(EXPERTS, dtype=jnp.int32)[None, None, :]
    onehot = (expert_match & used_mask[:, :, None]).astype(jnp.int32)
    ordered = jnp.transpose(onehot, (1, 0, 2)).reshape(TOPMAX * row_count, EXPERTS)
    before = jnp.cumsum(ordered, axis=0, dtype=jnp.int32) - ordered
    slot_index = jnp.sum(before * ordered, axis=1, dtype=jnp.int32).reshape(TOPMAX, row_count).T
    kept_mask = used_mask & (slot_index < CAP)
    position = jnp.where(kept_mask, expert_ids * CAP + slot_index, EXPERTS * CAP)
    entries = jnp.full((EXPERTS * CAP + 1,), row_count * TOPMAX, jnp.int32)
    entries = entries.at[position.reshape(-1)].set(jnp.arange(row_count * TOPMAX, dtype=jnp.int32))
    return (position, kept_mask.astype(jnp.float32), entries[: EXPERTS * CAP])


def block_span():
    return min(512, GRID)


def masked_scores(query_block, key_rows, live_keys, score_scale):
    scores = (
        jnp.einsum("qhd,khd->hqk", query_block, key_rows, preferred_element_type=jnp.float32)
        * score_scale
    )
    return jnp.where(live_keys[None, None, :] > 0, scores, NEGATIVE)


def attend_forward(query, key_rows, value_rows, live_keys, score_scale):
    blocks = query.reshape(GRID // block_span(), block_span(), HEADS, HEAD_DIM)

    def block_step(query_block):
        scores = masked_scores(query_block, key_rows, live_keys, score_scale)
        row_max = jnp.max(scores, axis=-1, keepdims=True)
        raised = jnp.exp(scores - row_max)
        row_total = jnp.sum(raised, axis=-1, keepdims=True)
        weights = (raised / row_total).astype(jnp.bfloat16)
        produced = jnp.einsum(
            "hqk,khd->qhd", weights, value_rows, preferred_element_type=jnp.float32
        )
        return (produced, row_max, row_total)

    produced, maxima, totals = lax.map(block_step, blocks)
    return (produced.reshape(GRID, HEADS, HEAD_DIM).astype(jnp.bfloat16), maxima, totals)


def attend_backward(query, key_rows, value_rows, live_keys, maxima, totals, upstream, score_scale):
    count = GRID // block_span()
    blocks = query.reshape(count, block_span(), HEADS, HEAD_DIM)
    grad_blocks = upstream.reshape(count, block_span(), HEADS, HEAD_DIM)

    def block_step(running, pieces):
        query_block, grad_block, row_max, row_total = pieces
        scores = masked_scores(query_block, key_rows, live_keys, score_scale)
        weights = jnp.exp(scores - row_max) / row_total
        dweights = jnp.einsum(
            "qhd,khd->hqk", grad_block, value_rows, preferred_element_type=jnp.float32
        )
        inner_sum = jnp.sum(dweights * weights, axis=-1, keepdims=True)
        dscores = (weights * (dweights - inner_sum)).astype(jnp.bfloat16)
        dquery = (
            jnp.einsum("hqk,khd->qhd", dscores, key_rows, preferred_element_type=jnp.float32)
            * score_scale
        )
        dkeys = (
            running[0]
            + jnp.einsum("hqk,qhd->khd", dscores, query_block, preferred_element_type=jnp.float32)
            * score_scale
        )
        dvalues = running[1] + jnp.einsum(
            "hqk,qhd->khd",
            weights.astype(jnp.bfloat16),
            grad_block,
            preferred_element_type=jnp.float32,
        )
        return ((dkeys, dvalues), dquery)

    zero_rows = jnp.zeros((GRID, HEADS, HEAD_DIM), jnp.float32)
    (dkeys, dvalues), dquery = lax.scan(
        block_step, (zero_rows, zero_rows), (blocks, grad_blocks, maxima, totals)
    )
    return jnp.stack([dquery.reshape(GRID, HEADS, HEAD_DIM), dkeys, dvalues], axis=1)


def run_experts(dispatched, expert_pair):
    pre_gelu = jnp.einsum(
        "ecd,edf->ecf", dispatched, expert_pair[0], preferred_element_type=jnp.float32
    )
    hidden = jax.nn.gelu(pre_gelu).astype(jnp.bfloat16)
    result = jnp.einsum("ecf,efd->ecd", hidden, expert_pair[1], preferred_element_type=jnp.float32)
    return (result.astype(jnp.bfloat16), (dispatched, pre_gelu, hidden))


def experts_back(dresult, expert_state, expert_pair):
    inputs_seen, pre_gelu, hidden = expert_state
    _, gelu_back = jax.vjp(jax.nn.gelu, pre_gelu)
    grad_out_term = jnp.einsum("ecf,ecd->efd", hidden, dresult, preferred_element_type=jnp.float32)
    dhidden = jnp.einsum(
        "ecd,efd->ecf", dresult, expert_pair[1], preferred_element_type=jnp.float32
    )
    dpre = gelu_back(dhidden)[0].astype(jnp.bfloat16)
    grad_in_term = jnp.einsum("ecd,ecf->edf", inputs_seen, dpre, preferred_element_type=jnp.float32)
    ddispatched = jnp.einsum(
        "ecf,edf->ecd", dpre, expert_pair[0], preferred_element_type=jnp.float32
    )
    return (ddispatched, grad_in_term, grad_out_term)


def forward_micro(tokens, valid, task_ids, top_counts, expert_ids, dense, expert_pair):
    attn_gain, attn_shift, proj_in, proj_out, moe_gain, moe_shift, router = dense
    row_count = tokens.shape[0]
    images = valid.shape[0]
    score_scale = 1.0 / math.sqrt(HEAD_DIM)
    inputs = tokens.astype(jnp.float32)
    normed_a, unit_a, inverse_a = normalize(inputs, attn_gain, attn_shift)
    normed_a = normed_a.astype(jnp.bfloat16)
    mixed = jnp.dot(normed_a, proj_in, preferred_element_type=jnp.float32).astype(jnp.bfloat16)
    head_parts = mixed.reshape(images, GRID, 3, HEADS, HEAD_DIM)
    queries = head_parts[:, :, 0]
    key_rows = head_parts[:, :, 1]
    value_rows = head_parts[:, :, 2]
    attended, maxima, totals = lax.map(
        lambda group: attend_forward(group[0], group[1], group[2], group[3], score_scale),
        (queries, key_rows, value_rows, valid),
    )
    attended = attended.reshape(row_count, D)
    resid = inputs + jnp.dot(attended, proj_out, preferred_element_type=jnp.float32)
    normed_b, unit_b, inverse_b = normalize(resid, moe_gain, moe_shift)
    normed_b = normed_b.astype(jnp.bfloat16)
    task_rows = jnp.repeat(task_ids, GRID)
    task_hot = (task_rows[:, None] == jnp.arange(TASKS, dtype=jnp.int32)[None, :]).astype(
        jnp.float32
    )
    router_flat = jnp.transpose(router, (1, 0, 2)).reshape(D, TASKS * EXPERTS)
    every_logit = jnp.dot(normed_b, router_flat, preferred_element_type=jnp.float32)
    logits = jnp.sum(every_logit.reshape(row_count, TASKS, EXPERTS) * task_hot[:, :, None], axis=1)
    raised = jnp.exp(logits - jnp.max(logits, axis=-1, keepdims=True))
    router_probs = raised / jnp.sum(raised, axis=-1, keepdims=True)
    position, kept_mask, entries = route(valid, task_ids, top_counts, expert_ids)
    onehot = (expert_ids[:, :, None] == jnp.arange(EXPERTS, dtype=jnp.int32)[None, None, :]).astype(
        jnp.float32
    )
    gate_values = jnp.sum(router_probs[:, None, :] * onehot, axis=-1) * kept_mask
    padded = jnp.concatenate([normed_b, jnp.zeros((1, D), jnp.bfloat16)], axis=0)
    dispatched = padded[entries // TOPMAX].reshape(EXPERTS, CAP, D)
    result, expert_state = run_experts(dispatched, expert_pair)
    result_rows = jnp.concatenate(
        [result.reshape(EXPERTS * CAP, D), jnp.zeros((1, D), jnp.bfloat16)], axis=0
    )
    picked = result_rows[position].astype(jnp.float32)
    output = resid + jnp.sum(gate_values[:, :, None] * picked, axis=1)
    kept_state = (
        unit_a,
        inverse_a,
        normed_a,
        queries,
        key_rows,
        value_rows,
        maxima,
        totals,
        attended,
        unit_b,
        inverse_b,
        normed_b,
        task_hot,
        router_probs,
        onehot,
        gate_values,
        position,
        kept_mask,
        entries,
        expert_state,
        result_rows,
    )
    return (output.astype(jnp.bfloat16), kept_state)


def backward_micro(cotangent, valid, kept_state, dense, expert_pair):
    attn_gain, attn_shift, proj_in, proj_out, moe_gain, moe_shift, router = dense
    (
        unit_a,
        inverse_a,
        normed_a,
        queries,
        key_rows,
        value_rows,
        maxima,
        totals,
        attended,
        unit_b,
        inverse_b,
        normed_b,
        task_hot,
        router_probs,
        onehot,
        gate_values,
        position,
        kept_mask,
        entries,
        expert_state,
        result_rows,
    ) = kept_state
    row_count = cotangent.shape[0]
    images = valid.shape[0]
    score_scale = 1.0 / math.sqrt(HEAD_DIM)
    upstream = cotangent.astype(jnp.float32)
    padded_grad = jnp.concatenate([upstream, jnp.zeros((1, D), jnp.float32)], axis=0)
    slot_gate = jnp.concatenate([gate_values.reshape(-1), jnp.zeros((1,), jnp.float32)], axis=0)[
        entries
    ]
    dresult = (
        (slot_gate[:, None] * padded_grad[entries // TOPMAX])
        .astype(jnp.bfloat16)
        .reshape(EXPERTS, CAP, D)
    )
    picked = result_rows[position].astype(jnp.float32)
    dgates = jnp.sum(upstream[:, None, :] * picked, axis=-1) * kept_mask
    ddispatched, grad_in_term, grad_out_term = experts_back(dresult, expert_state, expert_pair)
    ddispatched = jnp.concatenate(
        [ddispatched.reshape(EXPERTS * CAP, D), jnp.zeros((1, D), jnp.float32)], axis=0
    )
    dnormed_b = jnp.sum(ddispatched[position], axis=1)
    dprobs = jnp.sum(dgates[:, :, None] * onehot, axis=1)
    dlogits = router_probs * (dprobs - jnp.sum(dprobs * router_probs, axis=-1, keepdims=True))
    placed = (
        (dlogits[:, None, :] * task_hot[:, :, None])
        .astype(jnp.bfloat16)
        .reshape(row_count, TASKS * EXPERTS)
    )
    router_flat = jnp.transpose(router, (1, 0, 2)).reshape(D, TASKS * EXPERTS)
    grad_router = jnp.dot(normed_b.T, placed, preferred_element_type=jnp.float32)
    grad_router = jnp.transpose(grad_router.reshape(D, TASKS, EXPERTS), (1, 0, 2))
    dnormed_b = dnormed_b + jnp.dot(placed, router_flat.T, preferred_element_type=jnp.float32)
    dresid, grad_moe_gain, grad_moe_shift = normalize_back(dnormed_b, unit_b, inverse_b, moe_gain)
    dresid = upstream + dresid
    dbranch = dresid.astype(jnp.bfloat16)
    grad_proj_out = jnp.dot(attended.T, dbranch, preferred_element_type=jnp.float32)
    dattended = jnp.dot(dbranch, proj_out.T, preferred_element_type=jnp.float32).astype(
        jnp.bfloat16
    )
    dattended = dattended.reshape(images, GRID, HEADS, HEAD_DIM)
    dparts = lax.map(
        lambda group: attend_backward(*group, score_scale),
        (queries, key_rows, value_rows, valid, maxima, totals, dattended),
    )
    dmixed = dparts.reshape(row_count, 3 * D).astype(jnp.bfloat16)
    grad_proj_in = jnp.dot(normed_a.T, dmixed, preferred_element_type=jnp.float32)
    dnormed_a = jnp.dot(dmixed, proj_in.T, preferred_element_type=jnp.float32)
    dinputs, grad_attn_gain, grad_attn_shift = normalize_back(
        dnormed_a, unit_a, inverse_a, attn_gain
    )
    grad_tokens = (dresid + dinputs).astype(jnp.bfloat16)
    terms = (
        grad_attn_gain,
        grad_attn_shift,
        grad_proj_in,
        grad_proj_out,
        grad_moe_gain,
        grad_moe_shift,
        grad_router,
        grad_in_term,
        grad_out_term,
    )
    return (grad_tokens, terms)


def body(
    tokens,
    cotangent,
    valid,
    task_ids,
    top_counts,
    expert_ids,
    attn_gain,
    attn_shift,
    proj_in,
    proj_out,
    moe_gain,
    moe_shift,
    router,
    expert_in,
    expert_out,
):
    every = (
        lax.all_gather(attn_gain, "wide", axis=0, tiled=True),
        lax.all_gather(attn_shift, "wide", axis=0, tiled=True),
        lax.all_gather(proj_in, "wide", axis=0, tiled=True),
        lax.all_gather(proj_out, "wide", axis=0, tiled=True),
        lax.all_gather(moe_gain, "wide", axis=0, tiled=True),
        lax.all_gather(moe_shift, "wide", axis=0, tiled=True),
        lax.all_gather(router, "wide", axis=1, tiled=True),
        lax.all_gather(expert_in, "wide", axis=1, tiled=True),
        lax.all_gather(expert_out, "wide", axis=1, tiled=True),
    )
    dense = tuple(every[:7])
    expert_pair = (every[7], every[8])
    micro_rows = tokens.shape[0] // MICRO
    micro_images = valid.shape[0] // MICRO
    outputs = []
    states = []
    for micro_index in range(MICRO):
        row_start = micro_index * micro_rows
        image_start = micro_index * micro_images
        produced, kept_state = forward_micro(
            tokens[row_start : row_start + micro_rows],
            valid[image_start : image_start + micro_images],
            task_ids[image_start : image_start + micro_images],
            top_counts,
            expert_ids[row_start : row_start + micro_rows],
            dense,
            expert_pair,
        )
        outputs.append(produced)
        states.append(kept_state)
    every = (
        lax.all_gather(attn_gain, "wide", axis=0, tiled=True),
        lax.all_gather(attn_shift, "wide", axis=0, tiled=True),
        lax.all_gather(proj_in, "wide", axis=0, tiled=True),
        lax.all_gather(proj_out, "wide", axis=0, tiled=True),
        lax.all_gather(moe_gain, "wide", axis=0, tiled=True),
        lax.all_gather(moe_shift, "wide", axis=0, tiled=True),
        lax.all_gather(router, "wide", axis=1, tiled=True),
        lax.all_gather(expert_in, "wide", axis=1, tiled=True),
        lax.all_gather(expert_out, "wide", axis=1, tiled=True),
    )
    dense = tuple(every[:7])
    expert_pair = (every[7], every[8])
    grad_rows = []
    accumulated = None
    for micro_index in range(MICRO):
        row_start = micro_index * micro_rows
        image_start = micro_index * micro_images
        grad_tokens, terms = backward_micro(
            cotangent[row_start : row_start + micro_rows],
            valid[image_start : image_start + micro_images],
            states[micro_index],
            dense,
            expert_pair,
        )
        grad_rows.append(grad_tokens)
        accumulated = terms if micro_index == 0 else jax.tree.map(jnp.add, accumulated, terms)
    shares = (
        lax.psum_scatter(accumulated[0], "wide", scatter_dimension=0, tiled=True),
        lax.psum_scatter(accumulated[1], "wide", scatter_dimension=0, tiled=True),
        lax.psum_scatter(accumulated[2], "wide", scatter_dimension=0, tiled=True),
        lax.psum_scatter(accumulated[3], "wide", scatter_dimension=0, tiled=True),
        lax.psum_scatter(accumulated[4], "wide", scatter_dimension=0, tiled=True),
        lax.psum_scatter(accumulated[5], "wide", scatter_dimension=0, tiled=True),
        lax.psum_scatter(accumulated[6], "wide", scatter_dimension=1, tiled=True),
        lax.psum_scatter(accumulated[7], "wide", scatter_dimension=1, tiled=True),
        lax.psum_scatter(accumulated[8], "wide", scatter_dimension=1, tiled=True),
    )
    summed = lax.psum(
        (
            shares[0],
            shares[1],
            shares[2],
            shares[3],
            shares[4],
            shares[5],
            shares[6],
            shares[7],
            shares[8],
        ),
        "narrow",
    )
    return (
        jnp.concatenate(outputs, axis=0),
        jnp.concatenate(grad_rows, axis=0),
        summed[0],
        summed[1],
        summed[2],
        summed[3],
        summed[4],
        summed[5],
        summed[6],
        summed[7],
        summed[8],
    )


def solution(mesh):
    placed = (
        P(("narrow", "wide"), None),
        P(("narrow", "wide"), None),
        P(("narrow", "wide"), None),
        P(("narrow", "wide")),
        P(),
        P(("narrow", "wide"), None),
        P("wide"),
        P("wide"),
        P("wide", None),
        P("wide", None),
        P("wide"),
        P("wide"),
        P(None, "wide", None),
        P(None, "wide", None),
        P(None, "wide", None),
    )
    return jax.shard_map(
        body,
        mesh=mesh,
        in_specs=placed,
        out_specs=(
            P(("narrow", "wide"), None),
            P(("narrow", "wide"), None),
            P("wide"),
            P("wide"),
            P("wide", None),
            P("wide", None),
            P("wide"),
            P("wide"),
            P(None, "wide", None),
            P(None, "wide", None),
            P(None, "wide", None),
        ),
        check_vma=False,
    )
```

profile of v0, /device:TPU:0, one launch (start us, length us, event | category | flops | bytes accessed | tf_op | source)
XLA Modules:
  0.0 1288.6 jit_solution(5899042719771999554)
XLA Ops:
  16.4 35.8 %all-reduce.22 = (bf16[384]{0:T(512)(128)(2,1)S(1)}, bf16[384]{0:T(512)(128)(2,1)S(1)}, bf16[384]{0:T(512)(128)(2,1)S(1)}, bf16[384]{0:T(512)(128)(2,1)S(1)}) all-reduce(bf16[384]{0:T(512)(128)(2,1)S(1)} %dynamic-update-slice.1, bf16[384]{0:T(512)(128)(2,1)S(1)} %dynamic-update-slice, ...), channel_id=1, replica_groups=mesh['narrow'=2,'wide'=16] {'wide'}, use_global_device_ids=true, to_apply=%add.9 | all-reduce | flops 1536 | bytes 6144
  68.5 18.6 %all_gather.40 = bf16[2,384,8]{2,0,1:T(2,128)(2,1)S(1)} all-gather(bf16[2,24,8]{2,0,1:T(2,128)(2,1)S(1)} %copy.145), channel_id=1, replica_groups=mesh['narrow'=2,'wide'=16] {'wide'}, dimensions={1}, use_global_device_ids=true | all-gather | bytes 13056 | tf_op jit(solution)/shard_map/all_gather | solution.py:331
  87.8 21.8 %all_gather.36 = bf16[384,1152]{1,0:T(8,128)(2,1)S(1)} all-gather(bf16[24,1152]{1,0:T(8,128)(2,1)S(1)} %copy-done.113), channel_id=1, replica_groups=mesh['narrow'=2,'wide'=16] {'wide'}, dimensions={0}, use_global_device_ids=true | all-gather | bytes 940032 | tf_op jit(solution)/shard_map/all_gather | solution.py:327
  120.5 18.0 %while.99 = (s32[]{:T(128)}, bf16[2,512,6,64]{1,3,2,0:T(8,128)(2,1)S(1)}, f32[2,6,512,1]{2,1,3,0:T(8,128)S(1)}, f32[2,6,512,1]{2,1,3,0:T(8,128)S(1)}, s32[1024]{...) while((s32[]{:T(128)}, ...), condition=%wide.region_23.24_spmd, body=%wide.region_20.23_spmd.sunk | while | flops 843049984 | bytes 40644720 | solution.py:83
  153.9 20.1 %while.98 = (s32[]{:T(128)}, bf16[2,512,6,64]{1,3,2,0:T(8,128)(2,1)}, f32[2,6,512,1]{2,1,3,0:T(8,128)S(1)}, f32[2,6,512,1]{2,1,3,0:T(8,128)S(1)}, s32[1024]{0:T(...) while((s32[]{:T(128)}, ...), condition=%wide.region_5.6_spmd, body=%wide.region_2.5_spmd.sunk | while | flops 843049984 | bytes 46936232 | solution.py:83
  177.6 19.6 %all_gather.37 = bf16[384,384]{1,0:T(8,128)(2,1)S(1)} all-gather(bf16[24,384]{1,0:T(8,128)(2,1)S(1)} %copy-done.122), channel_id=1, replica_groups=mesh['narrow'=2,'wide'=16] {'wide'}, dimensions={0}, use_global_device_ids=true | all-gather | bytes 313344 | tf_op jit(solution)/shard_map/all_gather | solution.py:328
  210.4 15.5 %scatter_custom_fusion.1 = s32[2049]{0:T(1024)S(1)} fusion(s32[4096]{0:T(1024)S(1)} %bitcast.444, s32[4096]{0:T(1024)S(1)} %iota.65, s32[]{:T(128)} %constant.234.clone.1), kind=kCustom, calls=%fused_computation.341 | custom fusion | bytes 8200 | tf_op jit(solution)/shard_map/scatter | solution.py:53
  225.9 12.0 gather_fusion.7
  238.5 15.5 %scatter_custom_fusion = s32[2049]{0:T(1024)S(1)} fusion(s32[4096]{0:T(1024)S(1)} %bitcast.443, s32[4096]{0:T(1024)S(1)} %iota.63, s32[]{:T(128)} %constant.234.clone.1), kind=kCustom, calls=%fused_computation.343 | custom fusion | bytes 8200 | tf_op jit(solution)/shard_map/scatter | solution.py:53
  254.1 11.8 gather_fusion.4
  266.1 9.1 gather_fusion
  277.8 8.7 gather_fusion.5
  286.5 7.4 gather_fusion.2
  296.1 8.7 gather_fusion.8
  305.4 10.1 fusion.193
  315.5 10.3 convolution_convert_fusion.2
  326.0 17.0 %gather_fusion.3 = bf16[4096,384]{1,0:T(8,128)(2,1)} fusion(bf16[2049,384]{1,0:T(8,128)(2,1)S(1)} %concatenate.39, s32[4096]{0:T(1024)S(1)} %broadcast_clamp_fusion), kind=kCustom, calls=%fused_computation.3 | custom fusion | bytes 6307840 | tf_op jit(solution)/shard_map/gather | solution.py:190
  343.1 6.8 reshape.782
  349.9 14.7 %multiply_reduce_fusion.2 = (f32[1024,4]{1,0:T(8,128)}, f32[1024,384]{1,0:T(8,128)}) fusion(f32[1024,4,384]{2,1,0:T(4,128)} %reshape.782, f32[1024,384]{1,0:T(8,128)} %get-tuple-element.738, f32[1024,4]{1,0:T(8,128)} %copy-done.57), kind=kLoop, calls=%fused_computation.120 | loop fusion | flops 5894144 | bytes 9469952 | tf_op jit(solution)/shard_map/reduce_sum | solution.py:257
  366.5 17.2 %fusion.73 = bf16[8,256,1536]{2,1,0:T(8,128)(2,1)} fusion(f32[8,256,1536]{2,1,0:T(8,128)} %fusion.193, bf16[8,1536,384]{2,1,0:T(8,128)(2,1)} %all-gather.5.cloned.1.call-done, f32[8,256,384]{2,1,0:T(8,128)S(1)} %bitcast.412, f32[8,256]{1,0:T(8,128)S(1)} %mul.576), kind=kOutput, calls=%fused_computation.115 | convolution fusion | flops 2480406528 | bytes 31465472 | tf_op jit(solution)/shard_map/ecd,efd->ecf/dot_general | solution.py:138
  383.8 10.4 fusion.195
  394.4 16.4 %gather_fusion.9 = f32[4096,384]{1,0:T(8,128)} fusion(f32[2049,384]{1,0:T(8,128)S(1)} %concatenate.46, s32[4096]{0:T(1024)S(1)} %broadcast_clamp_fusion), kind=kCustom, calls=%fused_computation.9 | custom fusion | bytes 12599296 | tf_op jit(solution)/shard_map/gather | solution.py:262
  410.8 7.6 reshape.748
  424.9 10.7 convolution_convert_fusion.3
  436.9 10.8 fusion.112
  447.7 17.9 %fusion.66 = bf16[8,256,1536]{2,1,0:T(8,128)(2,1)} fusion(f32[8,256,1536]{2,1,0:T(8,128)} %copy-done.36, bf16[8,1536,384]{2,1,0:T(8,128)(2,1)} %all-gather.5.cloned.1.call-done, f32[8,256,384]{2,1,0:T(8,128)} %bitcast.428, f32[8,256]{1,0:T(8,128)S(1)} %mul.544), kind=kOutput, calls=%fused_computation.108 | convolution fusion | flops 2480406528 | bytes 31465472 | tf_op jit(solution)/shard_map/ecd,efd->ecf/dot_general | solution.py:138
  465.6 10.3 fusion.194
  476.6 18.3 %gather_fusion.1 = bf16[4096,384]{1,0:T(8,128)(2,1)} fusion(bf16[2049,384]{1,0:T(8,128)(2,1)} %concatenate.37, s32[4096]{0:T(1024)S(1)} %copy-done.8), kind=kCustom, calls=%fused_computation.1 | custom fusion | bytes 6307840 | tf_op jit(solution)/shard_map/gather | solution.py:190
  494.9 16.4 %gather_fusion.6 = f32[4096,384]{1,0:T(8,128)} fusion(f32[2049,384]{1,0:T(8,128)S(1)} %concatenate.43, s32[4096]{0:T(1024)S(1)} %copy-done.8), kind=kCustom, calls=%fused_computation.6 | custom fusion | bytes 12599296 | tf_op jit(solution)/shard_map/gather | solution.py:262
  511.3 7.6 reshape.724
  518.9 6.9 reshape.781
  525.9 14.5 %multiply_reduce_fusion.3 = (f32[1024,4]{1,0:T(8,128)S(1)}, f32[1024,384]{1,0:T(8,128)}) fusion(f32[1024,4,384]{2,1,0:T(4,128)} %reshape.781, f32[1024,384]{1,0:T(8,128)S(1)} %copy-done.41, f32[1024,4]{1,0:T(8,128)S(1)} %copy-done.56), kind=kLoop, calls=%fused_computation.121 | loop fusion | flops 5894144 | bytes 9469952 | tf_op jit(solution)/shard_map/reduce_sum | solution.py:257
  540.9 6.5 reduce_sum.460
  549.1 7.8 reduce_sum.452
  576.4 43.1 %while.100 = (s32[]{:T(128)}, f32[1024,6,64]{0,2,1:T(8,128)S(1)}, f32[1024,6,64]{0,2,1:T(8,128)}, bf16[2,512,6,64]{1,3,2,0:T(8,128)(2,1)}, bf16[2,512,6,64]{1,3,...) while((s32[]{:T(128)}, f32[1024,6,64]{0,2,1:T(8,128)S(1)}, ...), condition=%wide.region_44.45_spmd.clone, body=%wide.region_42.44_spmd.clone.sunk | while | flops 2046883840 | bytes 130652504 | solution.py:119
  582.5 6.5 multiply_reduce_fusion.20
  604.1 6.5 multiply_reduce_fusion.20
  635.6 43.3 %while.101 = (s32[]{:T(128)}, f32[1024,6,64]{0,2,1:T(8,128)S(1)}, f32[1024,6,64]{0,2,1:T(8,128)}, bf16[2,512,6,64]{1,3,2,0:T(8,128)(2,1)}, bf16[2,512,6,64]{1,3,...) while((s32[]{:T(128)}, f32[1024,6,64]{0,2,1:T(8,128)S(1)}, ...), condition=%wide.region_55.56_spmd.clone, body=%wide.region_53.55_spmd.clone.sunk | while | flops 2046883840 | bytes 130652504 | solution.py:119
  641.7 6.5 multiply_reduce_fusion.21
  663.2 6.5 multiply_reduce_fusion.21
  691.5 19.8 %convolution_add_fusion = f32[8,1536,384]{2,1,0:T(8,128)} fusion(f32[8,1536,384]{2,1,0:T(8,128)} %fusion.112, f32[8,256,384]{2,1,0:T(8,128)} %bitcast.411, f32[8,256]{1,0:T(8,128)S(1)} %copy-done.95, f32[8,256,1536]{2,1,0:T(8,128)} %fusion.193), kind=kOutput, calls=%fused_computation.118 | convolution fusion | flops 2450522112 | bytes 53485568 | tf_op jit(solution)/shard_map/ecf,ecd->efd/dot_general | solution.py:137
  712.8 12.0 fusion.197
  724.8 17.6 %convolution_add_fusion.1 = f32[8,384,1536]{2,1,0:T(8,128)} fusion(f32[8,384,1536]{2,1,0:T(8,128)} %fusion.197, bf16[8,256,384]{2,1,0:T(8,128)(2,1)S(1)} %bitcast.416, bf16[8,256,1536]{2,1,0:T(8,128)(2,1)} %fusion.73), kind=kOutput, calls=%fused_computation.119 | convolution fusion | flops 2420637696 | bytes 45613056 | tf_op jit(solution)/shard_map/ecd,ecf->edf/dot_general | solution.py:142
  756.0 191.0 %reduce-scatter.12.cloned.1.call-done = f32[8,96,384]{2,1,0:T(8,128)} async-done(((f32[8,1536,384]{2,1,0:T(8,128)}), f32[8,96,384]{2,1,0:T(8,128)}) %reduce-scatter.12.cloned.1.call-update) | async-done | bytes 1179664 | tf_op jit(solution)/shard_map/reduce_scatter | solution.py:391
  947.0 197.9 %reduce-scatter.10.cloned.1.call-done = f32[8,24,1536]{2,1,0:T(8,128)} async-done(((f32[8,384,1536]{2,1,0:T(8,128)}), f32[8,24,1536]{2,1,0:T(8,128)}) %reduce-scatter.10.cloned.1.call-update) | async-done | bytes 1179664 | tf_op jit(solution)/shard_map/reduce_scatter | solution.py:390
  1147.7 59.6 %all-reduce.19 = (f32[384]{0:T(512)S(1)}, f32[384]{0:T(512)S(1)}, f32[384]{0:T(512)S(1)}, f32[384]{0:T(512)S(1)}, f32[2,384,8]{1,2,0:T(8,128)S(1)}) all-reduce(f32[384]{0:T(512)S(1)} %add.308, f32[384]{0:T(512)S(1)} %add.309, f32[384]{0:T(512)S(1)} %add.312, f32[384]{0:T(512)S(1)} %add.313, ...), channel_id=2, replica_groups=mesh['narrow'=2,'wide'=16] {'wide'}, use_global_device_ids=true, to_apply=%region_60.61.clone | all-reduce | flops 7680 | bytes 61440
  1215.2 10.6 all-reduce.20
  1225.8 50.6 %all-reduce.25.cloned.1.call-done = (f32[24,1152]{1,0:T(8,128)}, f32[8,24,1536]{2,1,0:T(8,128)}, f32[8,96,384]{2,1,0:T(8,128)}) async-done(((f32[24,1152]{1,0:T(8,128)}, f32[8,24,1536]{2,1,0:T(8,128)}, f32[8,96,384]{2,1,0:T(8,128)}), (f32[24,1152]{1,0:T(8,128)}, f32[8,24,1536]{2,1,0:T(8,128)}, f32[8,96,384]{2,1,0:T(8,128)})) %all-reduce.25.cloned.1.call-update) | async-done | bytes 2469904 | tf_op jit(solution)/shard_map/psum | solution.py:393
  (598 shorter events, 261.1 us)
Async XLA Ops:
  7.2 55.9 %copy-start.29 = (bf16[2048,384]{1,0:T(8,128)(2,1)S(1)}, bf16[2048,384]{1,0:T(8,128)(2,1)}, u32[]{:S(2)}) copy-start(bf16[2048,384]{1,0:T(8,128)(2,1)} %param.23) | copy-start | bytes 4718596
  7.2 56.8 %copy-start.140 = (bf16[2,24,8]{1,2,0:T(8,128)(2,1)S(1)}, bf16[2,24,8]{1,2,0:T(8,128)(2,1)}, u32[]{:S(2)}) copy-start(bf16[2,24,8]{1,2,0:T(8,128)(2,1)} %param.35) | copy-start | bytes 2308
  7.2 56.9 %copy-start.99 = (s32[2048,4]{0,1:T(4,128)S(1)}, s32[2048,4]{0,1:T(4,128)}, u32[]{:S(2)}) copy-start(s32[2048,4]{0,1:T(4,128)} %param.28) | copy-start | bytes 98308
  7.2 80.6 %copy-start.113 = (bf16[24,1152]{1,0:T(8,128)(2,1)S(1)}, bf16[24,1152]{1,0:T(8,128)(2,1)}, u32[]{:S(2)}) copy-start(bf16[24,1152]{1,0:T(8,128)(2,1)} %param.31) | copy-start | bytes 165892
  7.2 298.2 %all-gather.3.cloned.1.call-start = ((), (), s32[]{:S(2)}) async-start(), calls=%async_computation.4 | async-start | bytes 10027008 | tf_op jit(solution)/shard_map/all_gather | solution.py:332
  8.0 307.6 %all-gather.5.cloned.1.call-start = ((), (), s32[]{:S(2)}) async-start(), calls=%async_computation.5 | async-start | bytes 10027008 | tf_op jit(solution)/shard_map/all_gather | solution.py:333
  8.7 747.3 %reduce-scatter.14.cloned.1.call-start = ((), (), s32[]{:S(2)}) async-start(), calls=%async_computation.8 | async-start | bytes 1880064
  52.2 87.3 %copy-start.141 = (f32[384]{0:T(512)}, f32[384]{0:T(512)S(1)}, u32[]{:S(2)}) copy-start(f32[384]{0:T(512)S(1)} %convert_element_type.202) | copy-start | bytes 4612
  58.2 81.3 %copy-start.137 = (f32[384]{0:T(512)}, f32[384]{0:T(512)S(1)}, u32[]{:S(2)}) copy-start(f32[384]{0:T(512)S(1)} %convert_element_type.201) | copy-start | bytes 4612
  63.0 50.5 %copy-start.114 = (f32[1024]{0:T(1024)}, f32[1024]{0:T(1024)S(1)}, u32[]{:S(2)}) copy-start(f32[1024]{0:T(1024)S(1)} %get-tuple-element.767) | copy-start | bytes 12292
  63.0 76.5 %copy-start.116 = (f32[1024]{0:T(1024)}, f32[1024]{0:T(1024)S(1)}, u32[]{:S(2)}) copy-start(f32[1024]{0:T(1024)S(1)} %get-tuple-element.768) | copy-start | bytes 12292
  64.0 75.6 %copy-start.123 = (f32[1024]{0:T(1024)}, f32[1024]{0:T(1024)S(1)}, u32[]{:S(2)}) copy-start(f32[1024]{0:T(1024)S(1)} %add_rsqrt_fusion.3) | copy-start | bytes 12292
  64.0 49.5 %copy-start.125 = (f32[1024]{0:T(1024)}, f32[1024]{0:T(1024)S(1)}, u32[]{:S(2)}) copy-start(f32[1024]{0:T(1024)S(1)} %add_rsqrt_fusion.1) | copy-start | bytes 12292
  141.0 56.1 %copy-start.48 = (bf16[48,8,2,512]{3,1,2,0:T(8,128)(2,1)}, bf16[48,8,2,512]{3,1,2,0:T(8,128)(2,1)S(1)}, u32[]{:S(2)}) copy-start(bf16[48,8,2,512]{3,1,2,0:T(8,128)(2,1)S(1)} %copy.182) | copy-start | bytes 2359300
  174.0 23.9 %copy-start.2 = (bf16[1024,6,64]{0,2,1:T(8,128)(2,1)}, bf16[1024,6,64]{0,2,1:T(8,128)(2,1)S(1)}, u32[]{:S(2)}) copy-start(bf16[1024,6,64]{0,2,1:T(8,128)(2,1)S(1)} %get-tuple-element.1195) | copy-start | bytes 2359300
  174.0 23.9 %copy-start.22 = (bf16[1024,6,64]{0,2,1:T(8,128)(2,1)}, bf16[1024,6,64]{0,2,1:T(8,128)(2,1)S(1)}, u32[]{:S(2)}) copy-start(bf16[1024,6,64]{0,2,1:T(8,128)(2,1)S(1)} %get-tuple-element.1201) | copy-start | bytes 2359300
  174.0 24.0 %copy-start.24 = (bf16[2,512,6,64]{1,3,2,0:T(8,128)(2,1)}, bf16[2,512,6,64]{1,3,2,0:T(8,128)(2,1)S(1)}, u32[]{:S(2)}) copy-start(bf16[2,512,6,64]{1,3,2,0:T(8,128)(2,1)S(1)} %get-tuple-element.1202) | copy-start | bytes 2359300
  174.0 24.0 %copy-start.78 = (s32[1024]{0:T(1024)}, s32[1024]{0:T(1024)S(1)}, u32[]{:S(2)}) copy-start(s32[1024]{0:T(1024)S(1)} %get-tuple-element.1216) | copy-start | bytes 12292
  174.0 24.0 %copy-start.84 = (f32[2,6,512,1]{2,1,3,0:T(8,128)}, f32[2,6,512,1]{2,1,3,0:T(8,128)S(1)}, u32[]{:S(2)}) copy-start(f32[2,6,512,1]{2,1,3,0:T(8,128)S(1)} %get-tuple-element.1138) | copy-start | bytes 73732
  174.0 24.0 %copy-start.86 = (f32[2,6,512,1]{2,1,3,0:T(8,128)}, f32[2,6,512,1]{2,1,3,0:T(8,128)S(1)}, u32[]{:S(2)}) copy-start(f32[2,6,512,1]{2,1,3,0:T(8,128)S(1)} %get-tuple-element.1137) | copy-start | bytes 73732
  174.1 23.1 %copy-start.31 = (bf16[2048,384]{1,0:T(8,128)(2,1)S(1)}, bf16[2048,384]{1,0:T(8,128)(2,1)}, u32[]{:S(2)}) copy-start(bf16[2048,384]{1,0:T(8,128)(2,1)} %param.23) | copy-start | bytes 4718596
  176.9 22.3 %copy-start.50 = (bf16[48,8,2,512]{3,1,2,0:T(8,128)(2,1)}, bf16[48,8,2,512]{3,1,2,0:T(8,128)(2,1)S(1)}, u32[]{:S(2)}) copy-start(bf16[48,8,2,512]{3,1,2,0:T(8,128)(2,1)S(1)} %copy.178) | copy-start | bytes 2359300
  177.6 23.2 %copy-start.143 = (f32[2]{0:T(128)}, f32[2]{0:T(128)S(1)}, u32[]{:S(2)}) copy-start(f32[2]{0:T(128)S(1)} %compare_convert_fusion.1) | copy-start | bytes 28
  200.7 65.2 %copy-start.44 = (bf16[1024,384]{1,0:T(8,128)(2,1)}, bf16[1024,384]{1,0:T(8,128)(2,1)S(1)}, u32[]{:S(2)}) copy-start(bf16[1024,384]{1,0:T(8,128)(2,1)S(1)} %get-tuple-element.751) | copy-start | bytes 2359300
  200.7 65.3 %copy-start.43 = (bf16[1024,384]{1,0:T(8,128)(2,1)}, bf16[1024,384]{1,0:T(8,128)(2,1)S(1)}, u32[]{:S(2)}) copy-start(bf16[1024,384]{1,0:T(8,128)(2,1)S(1)} %get-tuple-element.752) | copy-start | bytes 2359300
  237.9 128.6 %copy-start.94 = (f32[8,256]{1,0:T(8,128)}, f32[8,256]{1,0:T(8,128)S(1)}, u32[]{:S(2)}) copy-start(f32[8,256]{1,0:T(8,128)S(1)} %mul.576) | copy-start | bytes 24580
  294.0 11.4 copy-start.38
  349.9 16.7 %copy-start.35 = (f32[2048,384]{1,0:T(8,128)S(1)}, f32[2048,384]{1,0:T(8,128)}, u32[]{:S(2)}) copy-start(f32[2048,384]{1,0:T(8,128)} %gather_fusion.8) | copy-start | bytes 9437188
  424.9 12.0 copy-start.36
  525.9 14.8 %copy-start.119 = (pred[1024,4]{0,1:T(4,128)(4,1)S(1)}, pred[1024,4]{0,1:T(4,128)(4,1)}, u32[]{:S(2)}) copy-start(pred[1024,4]{0,1:T(4,128)(4,1)} %copy-done.118) | copy-start | bytes 12292
  525.9 14.8 %copy-start.98 = (s32[1024,4]{0,1:T(4,128)S(1)}, s32[1024,4]{0,1:T(4,128)}, u32[]{:S(2)}) copy-start(s32[1024,4]{0,1:T(4,128)} %get-tuple-element.744) | copy-start | bytes 49156
  525.9 14.8 %copy-start.71 = (f32[1024,8]{0,1:T(8,128)S(1)}, f32[1024,8]{0,1:T(8,128)}, u32[]{:S(2)}) copy-start(f32[1024,8]{0,1:T(8,128)} %copy-done.70) | copy-start | bytes 98308
  525.9 14.8 %copy-start.102 = (f32[1024]{0:T(1024)S(1)}, f32[1024]{0:T(1024)}, u32[]{:S(2)}) copy-start(f32[1024]{0:T(1024)} %copy-done.101) | copy-start | bytes 12292
  525.9 14.8 %copy-start.108 = (f32[1024]{0:T(1024)S(1)}, f32[1024]{0:T(1024)}, u32[]{:S(2)}) copy-start(f32[1024]{0:T(1024)} %copy-done.107) | copy-start | bytes 12292
  540.8 16.1 %copy-start.92 = (f32[1024,8]{0,1:T(8,128)}, f32[1024,8]{0,1:T(8,128)S(1)}, u32[]{:S(2)}) copy-start(f32[1024,8]{0,1:T(8,128)S(1)} %subtract_multiply_fusion.3) | copy-start | bytes 98308
  567.2 9.2 copy-start.3
  567.2 9.2 copy-start.5
  567.2 9.2 copy-start.23
  567.2 9.2 copy-start.79
  567.2 9.2 copy-start.85
  567.2 9.2 copy-start.87
  691.5 255.5 %reduce-scatter.12.cloned.1.call-start = ((), (), s32[]{:S(2)}) async-start(), calls=%async_computation.7 | async-start | bytes 20054016 | tf_op jit(solution)/shard_map/reduce_scatter | solution.py:391
  711.4 433.5 %reduce-scatter.10.cloned.1.call-start = ((), (), s32[]{:S(2)}) async-start(), calls=%async_computation.6 | async-start | bytes 20054016 | tf_op jit(solution)/shard_map/reduce_scatter | solution.py:390
  712.8 12.0 copy-start.39
  742.4 472.7 %reduce-scatter.16.cloned.1.call-start = ((), (), s32[]{:S(2)}) async-start(), calls=%async_computation.9 | async-start | bytes 626688
  747.8 528.6 %all-reduce.25.cloned.1.call-start = ((), (), s32[]{:S(2)}) async-start(), calls=%async_computation.10 | async-start | bytes 4939776 | tf_op jit(solution)/shard_map/psum | solution.py:393
  751.5 393.4 %copy-start.93 = (f32[1024,8]{0,1:T(8,128)S(1)}, f32[1024,8]{0,1:T(8,128)}, u32[]{:S(2)}) copy-start(f32[1024,8]{0,1:T(8,128)} %copy-done.92) | copy-start | bytes 98308
  755.9 390.4 %copy-start.91 = (f32[1024,8]{0,1:T(8,128)S(1)}, f32[1024,8]{0,1:T(8,128)}, u32[]{:S(2)}) copy-start(f32[1024,8]{0,1:T(8,128)} %subtract_multiply_fusion.2) | copy-start | bytes 98308
  (123 other events, 489.8 us)
Sparse Core Ops, SparseCore 0:
  10.3 86.9 all-gather.2
  99.6 80.2 all-gather.4
  691.6 57.4 reduce-scatter.13
  753.1 193.8 reduce-scatter.11
  951.0 193.8 reduce-scatter.9
  1148.3 53.9 reduce-scatter.15
  1204.9 71.4 all-reduce.24
where the time goes:
time: 1290 us
  waiting for transfers between devices  441 us (34%)
  matrix products  278 us (22%)
  local copies, waits for them, and re-layouts  269 us (21%)
  blocking collectives  166 us (13%)
  other arithmetic  114 us (9%)
  between operations  18.1 us (1%)
    reduce_scatter x1, waiting for transfers between devices, body(): lax.psum_scatter(accumulated[7], 'wide', scatter_dimension=1, tiled=True)  198 us
    reduce_scatter x1, waiting for transfers between devices, body(): lax.psum_scatter(accumulated[8], 'wide', scatter_dimension=1, tiled=True)  191 us
    unnamed x2, blocking collectives  95.4 us
    psum x1, waiting for transfers between devices, body(): lax.psum((shares[0], shares[1], shares[2], shares[3], shares[4], shares[5...  50.6 us
    gather x4, local copies, waits for them, and re-layouts, backward_micro(): dnormed_b = jnp.sum(ddispatched[position], axis=1)  48 us
    gather x2, local copies, waits for them, and re-layouts, forward_micro(): picked = result_rows[position].astype(jnp.float32)  35.3 us
    dot_general x2, matrix products, experts_back(): jnp.einsum('ecd,efd->ecf', dresult, expert_pair[1], preferred_element_typ...  35.1 us
    scatter x2, local copies, waits for them, and re-layouts, route(): entries.at[position.reshape(-1)]  31.1 us
  transfers between devices with their start and end apart: 7, of which 3 were waited for; matrix products, arithmetic and copies ran while one was open for 21% of the time, Pallas kernels for 0%

commit v1 on v0

v1 whole, which is shorter than its diff:
```python
import functools
import math

import jax
import jax.numpy as jnp
from jax import lax
from jax.experimental import pallas as pl
from jax.experimental.pallas import tpu as pltpu
from jax.sharding import PartitionSpec as P

D = 384
HEADS = 6
HEAD_DIM = 64
FF = 1536
EXPERTS = 8
TOPMAX = 4
TASKS = 2
GRID = 1024
CAP = 256
PAIRS = HEADS // 2
QB = 256
FC = 512
EPSILON = 1e-06
NEGATIVE = -1e30
SCALE = 1.0 / math.sqrt(HEAD_DIM)
MISC = 3 * D + D
DENSE = MISC + 128

F32 = jnp.float32
BF16 = jnp.bfloat16
VMEM_LIMIT = 60 * 1024 * 1024


def nn(a, b):
    return lax.dot_general(a, b, (((1,), (0,)), ((), ())), preferred_element_type=F32)


def nt(a, b):
    return lax.dot_general(a, b, (((1,), (1,)), ((), ())), preferred_element_type=F32)


def tn(a, b):
    return lax.dot_general(a, b, (((0,), (0,)), ((), ())), preferred_element_type=F32)


def lanes(shape):
    return lax.broadcasted_iota(jnp.int32, shape, 1)


def norm_rows(values):
    center = values - jnp.mean(values, axis=-1, keepdims=True)
    inverse = lax.rsqrt(jnp.mean(center * center, axis=-1, keepdims=True) + EPSILON)
    return center * inverse, inverse


def split3(value):
    high = value.astype(BF16).astype(F32)
    rest = value - high
    mid = rest.astype(BF16).astype(F32)
    return high, mid, rest - mid


def misc_rows(dense_ref):
    return dense_ref[:, MISC:].astype(F32).T


def router_of(dense_ref, task):
    block = dense_ref[:, MISC:].astype(F32)
    first = pltpu.roll(block, 128 - 4, 1)
    second = pltpu.roll(block, 128 - 12, 1)
    chosen = jnp.where(task == 0, first, second)
    return jnp.where(lanes(chosen.shape) < EXPERTS, chosen, 0.0).astype(BF16)


def column_of(row):
    return jnp.broadcast_to(row, (128, row.shape[1])).T


def forward_kernel(
    task_ref,
    count_ref,
    tokens_ref,
    valid_ref,
    ids_ref,
    dense_ref,
    mixed_ref,
    attended_ref,
    resid_ref,
    normed_ref,
    aux_ref,
    rows_ref,
    lse_ref,
    att_t,
):
    image = pl.program_id(0)
    task = task_ref[image]
    count = count_ref[task]
    misc = misc_rows(dense_ref)
    inputs = tokens_ref[...].astype(F32)
    unit_a, _ = norm_rows(inputs)
    normed_a = (unit_a * misc[0:1] + misc[1:2]).astype(BF16)
    mixed_ref[...] = nn(normed_a, dense_ref[:, : 3 * D]).astype(BF16)
    live_col = column_of(valid_ref[pl.ds(image, 1), :].astype(F32))
    lane = lanes((GRID, 128))
    key_ext = jnp.where((lane == 0) & (live_col < 0.5), NEGATIVE, 0.0).astype(BF16)
    query_ext = jnp.where(lanes((QB, 128)) == 0, 1.0, 0.0).astype(BF16)
    ones_rows = jnp.ones((16, GRID), BF16)

    def pair_step(pair, carry):
        at = pl.multiple_of(pair * 128, 128)
        keys = mixed_ref[:, pl.ds(D + at, 128)]
        values = mixed_ref[:, pl.ds(2 * D + at, 128)]
        key_full = jnp.concatenate([keys, key_ext], axis=1)
        value_t = jnp.concatenate([values.astype(F32).T.astype(BF16), ones_rows], axis=0)
        half = lanes((QB, 128)) // HEAD_DIM
        for block in range(GRID // QB):
            span = pl.ds(block * QB, QB)
            query = mixed_ref[span, pl.ds(at, 128)].astype(F32) * SCALE
            for part in range(2):
                own = jnp.where(half == part, query, 0.0).astype(BF16)
                scores = nt(key_full, jnp.concatenate([own, query_ext], axis=1))
                top = jnp.max(scores, axis=0, keepdims=True)
                raised = jnp.exp(scores - top).astype(BF16)
                produced = nn(value_t, raised)
                total = produced[128:129]
                mine = produced[part * HEAD_DIM : (part + 1) * HEAD_DIM] / total
                att_t[pl.ds(at + part * HEAD_DIM, HEAD_DIM), span] = mine
                lse_ref[0, pl.ds(pair * 2 + part, 1), span] = top + jnp.log(total)
        return carry

    lax.fori_loop(0, PAIRS, pair_step, 0)
    lse_ref[0, HEADS:, :] = jnp.zeros((8 - HEADS, GRID), F32)
    attended = att_t[...].T.astype(BF16)
    attended_ref[...] = attended
    resid = inputs + nn(attended, dense_ref[:, 3 * D : MISC])
    resid_ref[...] = resid
    unit_b, _ = norm_rows(resid)
    normed_b = (unit_b * misc[2:3] + misc[3:4]).astype(BF16)
    normed_ref[...] = normed_b
    logits = nn(normed_b, router_of(dense_ref, task))
    logits = jnp.where(lane < EXPERTS, logits, NEGATIVE)
    raised = jnp.exp(logits - jnp.max(logits, axis=-1, keepdims=True))
    probs = raised / jnp.sum(raised, axis=-1, keepdims=True)
    choice = lane // EXPERTS
    wanted = jnp.full((GRID, 128), -1, jnp.int32)
    for rank in range(TOPMAX):
        wanted = jnp.where(choice == rank, ids_ref[:, rank : rank + 1], wanted)
    used = (wanted == lane % EXPERTS) & (choice < count) & (live_col > 0.5)
    used = jnp.where(used, 1.0, 0.0)
    span = 256
    row_at = lax.broadcasted_iota(jnp.int32, (span, span), 0)
    earlier = jnp.where(row_at > lanes((span, span)), 1.0, 0.0).astype(BF16)
    running = jnp.zeros((1, 128), F32)
    pieces = []
    for block in range(GRID // span):
        part = used[block * span : (block + 1) * span]
        pieces.append(nn(earlier, part.astype(BF16)) + running)
        running = running + jnp.sum(part, axis=0, keepdims=True)
    before = jnp.concatenate(pieces, axis=0)
    totals = jnp.broadcast_to(running, (8, 128))
    lane8 = lanes((8, 128))
    base = jnp.zeros((8, 128), F32)
    for rank in range(1, TOPMAX):
        shift = rank * EXPERTS
        base = base + jnp.where(lane8 >= shift, pltpu.roll(totals, shift, 1), 0.0)
    slot = before + base[0:1]
    found = jnp.where((used > 0.5) & (slot < CAP), slot + 1.0, 0.0)
    folded = found
    for rank in range(1, TOPMAX):
        folded = folded + pltpu.roll(found, 128 - rank * EXPERTS, 1)
    slots = jnp.where(lane < EXPERTS, folded - 1.0, -1.0)
    gates = jnp.where(slots >= 0.0, probs, 0.0)
    aux = probs + jnp.where(
        (choice == 1), pltpu.roll(slots, EXPERTS, 1), 0.0
    ) + jnp.where(choice == 2, pltpu.roll(gates, 2 * EXPERTS, 1), 0.0)
    aux_ref[...] = aux
    rows_ref[0] = aux.T[0 : 4 * EXPERTS]


def forward_call(task_ids, top_counts, tokens, valid, expert_ids, dense):
    images = valid.shape[0]
    rows = images * GRID
    by_image = lambda width: pl.BlockSpec((GRID, width), lambda i, *_: (i, 0))
    whole = lambda shape: pl.BlockSpec(shape, lambda i, *_: (0,) * len(shape))
    lead = lambda shape: pl.BlockSpec((1,) + shape, lambda i, *_: (i, 0, 0))
    return pl.pallas_call(
        forward_kernel,
        grid_spec=pltpu.PrefetchScalarGridSpec(
            num_scalar_prefetch=2,
            grid=(images,),
            in_specs=[by_image(D), whole(valid.shape), by_image(TOPMAX), whole(dense.shape)],
            out_specs=[
                by_image(3 * D),
                by_image(D),
                by_image(D),
                by_image(D),
                by_image(128),
                lead((4 * EXPERTS, GRID)),
                lead((8, GRID)),
            ],
            scratch_shapes=[pltpu.VMEM((D, GRID), F32)],
        ),
        out_shape=[
            jax.ShapeDtypeStruct((rows, 3 * D), BF16),
            jax.ShapeDtypeStruct((rows, D), BF16),
            jax.ShapeDtypeStruct((rows, D), F32),
            jax.ShapeDtypeStruct((rows, D), BF16),
            jax.ShapeDtypeStruct((rows, 128), F32),
            jax.ShapeDtypeStruct((images, 4 * EXPERTS, GRID), F32),
            jax.ShapeDtypeStruct((images, 8, GRID), F32),
        ],
        compiler_params=pltpu.CompilerParams(vmem_limit_bytes=VMEM_LIMIT),
        name="attention_forward",
    )(task_ids, top_counts, tokens, valid, expert_ids, dense)


def expert_kernel(
    images,
    normed_ref,
    cot_ref,
    aux_ref,
    rows_ref,
    in_ref,
    out_ref,
    sums_ref,
    dprobs_ref,
    grad_in_ref,
    grad_out_ref,
    both,
    given,
    upstream,
    dres_s,
):
    expert = pl.program_id(0)

    @pl.when(expert == 0)
    def _():
        for image in range(images):
            span = pl.ds(image * GRID, GRID)
            both[span, :D] = normed_ref[span, :]
            both[span, D:] = cot_ref[span, :]

    slot_at = lax.broadcasted_iota(jnp.int32, (CAP, GRID), 0).astype(F32)
    for image in range(images):
        part = pl.ds(image * CAP, CAP)
        slot_row = rows_ref[image, pl.ds(EXPERTS + expert, 1), :]
        gate_row = rows_ref[image, pl.ds(2 * EXPERTS + expert, 1), :]
        match = slot_at == slot_row
        sent = nn(jnp.where(match, 1.0, 0.0).astype(BF16), both[pl.ds(image * GRID, GRID), :])
        gate = jnp.sum(jnp.where(match, gate_row, 0.0), axis=1, keepdims=True)
        given[part, :] = sent[:, :D].astype(BF16)
        upstream[part, :D] = sent[:, D:]
        upstream[part, D:] = jnp.broadcast_to(gate, (CAP, 128))
        dres_s[part, :] = (gate * sent[:, D:]).astype(BF16)
    slots = given[...]
    dres = dres_s[...]
    result = jnp.zeros((images * CAP, D), F32)
    back = jnp.zeros((images * CAP, D), F32)
    c1 = math.sqrt(2.0 / math.pi)
    c3 = c1 * 0.044715
    for chunk in range(FF // FC):
        span = pl.ds(chunk * FC, FC)
        w_in = in_ref[0, :, span]
        w_out = out_ref[0, span, :]
        pre = nn(slots, w_in)
        square = pre * pre
        curve = jnp.tanh(pre * (c1 + c3 * square))
        lifted = 0.5 * (1.0 + curve)
        hidden = (pre * lifted).astype(BF16)
        slope = lifted + (0.5 * pre) * (1.0 - curve * curve) * (c1 + (3.0 * c3) * square)
        result = result + nn(hidden, w_out)
        dpre = (nt(dres, w_out) * slope).astype(BF16)
        back = back + nt(dpre, w_in)
        grad_out_ref[0, span, :] = tn(hidden, dres).astype(grad_out_ref.dtype)
        grad_in_ref[0, :, span] = tn(slots, dpre).astype(grad_in_ref.dtype)
    result = result.astype(BF16).astype(F32)
    dgate = jnp.sum(result * upstream[:, :D], axis=1, keepdims=True)
    gated = result * upstream[:, D : D + 1]
    returned = jnp.concatenate([gated.astype(BF16), back.astype(BF16)], axis=1)
    for image in range(images):
        part = slice(image * CAP, (image + 1) * CAP)
        span = pl.ds(image * GRID, GRID)
        slot_row = rows_ref[image, pl.ds(EXPERTS + expert, 1), :]
        match = slot_at == slot_row
        dprobs_ref[image, pl.ds(expert, 1), :] = jnp.sum(
            jnp.where(match, dgate[part], 0.0), axis=0, keepdims=True
        )
        hit = jnp.where(match, 1.0, 0.0).astype(BF16)
        landed = tn(hit, returned[part])

        @pl.when(expert == 0)
        def _():
            sums_ref[span, :] = landed

        @pl.when(expert > 0)
        def _():
            sums_ref[span, :] = sums_ref[span, :] + landed


def expert_call(normed_b, cotangent, aux, rows, expert_in, expert_out):
    images = rows.shape[0]
    count = images * GRID
    whole = lambda shape: pl.BlockSpec(shape, lambda e: (0,) * len(shape))
    return pl.pallas_call(
        functools.partial(expert_kernel, images),
        grid=(EXPERTS,),
        in_specs=[
            whole((count, D)),
            whole((count, D)),
            whole((count, 128)),
            whole(rows.shape),
            pl.BlockSpec((1, D, FF), lambda e: (e, 0, 0)),
            pl.BlockSpec((1, FF, D), lambda e: (e, 0, 0)),
        ],
        out_specs=[
            whole((count, 2 * D)),
            whole((images, EXPERTS, GRID)),
            pl.BlockSpec((1, D, FF), lambda e: (e, 0, 0)),
            pl.BlockSpec((1, FF, D), lambda e: (e, 0, 0)),
        ],
        out_shape=[
            jax.ShapeDtypeStruct((count, 2 * D), F32),
            jax.ShapeDtypeStruct((images, EXPERTS, GRID), F32),
            jax.ShapeDtypeStruct((EXPERTS, D, FF), BF16),
            jax.ShapeDtypeStruct((EXPERTS, FF, D), BF16),
        ],
        scratch_shapes=[
            pltpu.VMEM((count, 2 * D), BF16),
            pltpu.VMEM((images * CAP, D), BF16),
            pltpu.VMEM((images * CAP, D + 128), F32),
            pltpu.VMEM((images * CAP, D), BF16),
        ],
        compiler_params=pltpu.CompilerParams(vmem_limit_bytes=VMEM_LIMIT),
        name="experts",
    )(normed_b, cotangent, aux, rows, expert_in, expert_out)


def norm_back(upstream, unit_rows, inverse, gain):
    scaled = upstream * gain
    centered = scaled - jnp.mean(scaled, axis=-1, keepdims=True)
    centered = centered - unit_rows * jnp.mean(scaled * unit_rows, axis=-1, keepdims=True)
    return inverse * centered


def backward_kernel(
    task_ref,
    tokens_ref,
    cot_ref,
    valid_ref,
    dense_ref,
    mixed_ref,
    attended_ref,
    resid_ref,
    normed_ref,
    aux_ref,
    lse_ref,
    sums_ref,
    dprobs_ref,
    output_ref,
    grad_tokens_ref,
    grad_dense_ref,
    grad_rows_ref,
    dmixed,
    dattended,
    acc_k,
    acc_v,
    dq_t,
):
    image = pl.program_id(0)
    task = task_ref[image]
    misc = misc_rows(dense_ref)
    lane = lanes((GRID, 128))
    upstream = cot_ref[...].astype(F32)
    resid = resid_ref[...]
    output_ref[...] = (resid + sums_ref[:, :D]).astype(BF16)
    unit_b, inverse_b = norm_rows(resid)
    probs = jnp.where(lane < EXPERTS, aux_ref[...], 0.0)
    dprobs = jnp.concatenate(
        [dprobs_ref[0], jnp.zeros((128 - EXPERTS, GRID), F32)], axis=0
    ).T
    dlogits = probs * (dprobs - jnp.sum(dprobs * probs, axis=-1, keepdims=True))
    dlogits = dlogits.astype(BF16)
    router = router_of(dense_ref, task)
    grad_router = tn(normed_ref[...], dlogits)
    dnormed_b = sums_ref[:, D:] + nt(dlogits, router)
    dresid = upstream + norm_back(dnormed_b, unit_b, inverse_b, misc[2:3])
    dbranch = dresid.astype(BF16)
    grad_proj_out = tn(attended_ref[...], dbranch)
    dattended[...] = nt(dbranch, dense_ref[:, 3 * D : MISC]).astype(BF16)
    live_col = column_of(valid_ref[pl.ds(image, 1), :].astype(F32))
    lse_col = jnp.concatenate([lse_ref[0], jnp.zeros((120, GRID), F32)], axis=0).T
    key_ext = jnp.where((lane == 0) & (live_col < 0.5), NEGATIVE, 0.0)
    key_ext = jnp.where((lane >= 1) & (lane <= 3), 1.0, key_ext).astype(BF16)
    value_ext = jnp.where(lane < 3, 1.0, 0.0).astype(BF16)
    small = lanes((QB, 128))
    half = small // HEAD_DIM

    def pair_step(pair, carry):
        at = pl.multiple_of(pair * 128, 128)
        keys = mixed_ref[:, pl.ds(D + at, 128)]
        values = mixed_ref[:, pl.ds(2 * D + at, 128)]
        key_full = jnp.concatenate([keys, key_ext], axis=1)
        value_full = jnp.concatenate([values, value_ext], axis=1)
        key_t = keys.astype(F32).T.astype(BF16)
        for block in range(GRID // QB):
            span = pl.ds(block * QB, QB)
            query = mixed_ref[span, pl.ds(at, 128)].astype(F32) * SCALE
            grad = dattended[span, pl.ds(at, 128)].astype(F32)
            seen = attended_ref[span, pl.ds(at, 128)].astype(F32) * grad
            for part in range(2):
                own = half == part
                inner = jnp.sum(jnp.where(own, seen, 0.0), axis=-1, keepdims=True)
                high, mid, low = split3(-inner)
                grad_ext = jnp.where(
                    small == 0, high, jnp.where(small == 1, mid, jnp.where(small == 2, low, 0.0))
                ).astype(BF16)
                head = pair * 2 + part
                shift = jnp.sum(
                    jnp.where(small == head, lse_col[block * QB : (block + 1) * QB], 0.0),
                    axis=-1,
                    keepdims=True,
                )
                high, mid, low = split3(-shift)
                query_ext = jnp.where(
                    small == 0,
                    1.0,
                    jnp.where(
                        small == 1, high, jnp.where(small == 2, mid, jnp.where(small == 3, low, 0.0))
                    ),
                ).astype(BF16)
                my_query = jnp.where(own, query, 0.0).astype(BF16)
                my_grad = jnp.where(own, grad, 0.0).astype(BF16)
                weights = jnp.exp(nt(key_full, jnp.concatenate([my_query, query_ext], axis=1)))
                drift = nt(value_full, jnp.concatenate([my_grad, grad_ext], axis=1))
                dscores = (weights * drift).astype(BF16)
                dkey = nn(dscores, my_query)
                dvalue = nn(weights.astype(BF16), my_grad)
                if block == 0 and part == 0:
                    acc_k[...] = dkey
                    acc_v[...] = dvalue
                else:
                    acc_k[...] += dkey
                    acc_v[...] += dvalue
                rows = slice(part * HEAD_DIM, (part + 1) * HEAD_DIM)
                dq_t[rows, span] = nn(key_t[rows], dscores)
        dmixed[:, pl.ds(at, 128)] = (dq_t[...].T * SCALE).astype(BF16)
        dmixed[:, pl.ds(D + at, 128)] = acc_k[...].astype(BF16)
        dmixed[:, pl.ds(2 * D + at, 128)] = acc_v[...].astype(BF16)
        return carry

    lax.fori_loop(0, PAIRS, pair_step, 0)
    unit_a, inverse_a = norm_rows(tokens_ref[...].astype(F32))
    normed_a = (unit_a * misc[0:1] + misc[1:2]).astype(BF16)
    grad_proj_in = tn(normed_a, dmixed[...])
    dnormed_a = nt(dmixed[...], dense_ref[:, : 3 * D])
    grad_tokens_ref[...] = (dresid + norm_back(dnormed_a, unit_a, inverse_a, misc[0:1])).astype(BF16)
    sums = [
        jnp.sum(dnormed_a * unit_a, axis=0, keepdims=True),
        jnp.sum(dnormed_a, axis=0, keepdims=True),
        jnp.sum(dnormed_b * unit_b, axis=0, keepdims=True),
        jnp.sum(dnormed_b, axis=0, keepdims=True),
        jnp.zeros((4, D), F32),
    ]
    sums = jnp.concatenate(sums, axis=0)
    placed = jnp.where(task == 0, pltpu.roll(grad_router, 4, 1), pltpu.roll(grad_router, 12, 1))

    @pl.when(image == 0)
    def _():
        grad_dense_ref[:, : 3 * D] = grad_proj_in
        grad_dense_ref[:, 3 * D : MISC] = grad_proj_out
        grad_dense_ref[:, MISC:] = placed
        grad_rows_ref[...] = sums

    @pl.when(image > 0)
    def _():
        grad_dense_ref[:, : 3 * D] += grad_proj_in
        grad_dense_ref[:, 3 * D : MISC] += grad_proj_out
        grad_dense_ref[:, MISC:] += placed
        grad_rows_ref[...] += sums

    @pl.when(image == pl.num_programs(0) - 1)
    def _():
        columns = jnp.concatenate([grad_rows_ref[...], jnp.zeros((120, D), F32)], axis=0).T
        keep = lanes((D, 128)) < 4
        grad_dense_ref[:, MISC:] = jnp.where(keep, columns, grad_dense_ref[:, MISC:])


def backward_call(
    task_ids, tokens, cotangent, valid, dense, mixed, attended, resid, normed_b, aux, lse, sums, dprobs
):
    images = valid.shape[0]
    rows = images * GRID
    by_image = lambda width: pl.BlockSpec((GRID, width), lambda i, *_: (i, 0))
    whole = lambda shape: pl.BlockSpec(shape, lambda i, *_: (0,) * len(shape))
    lead = lambda shape: pl.BlockSpec((1,) + shape, lambda i, *_: (i, 0, 0))
    return pl.pallas_call(
        backward_kernel,
        grid_spec=pltpu.PrefetchScalarGridSpec(
            num_scalar_prefetch=1,
            grid=(images,),
            in_specs=[
                by_image(D),
                by_image(D),
                whole(valid.shape),
                whole(dense.shape),
                by_image(3 * D),
                by_image(D),
                by_image(D),
                by_image(D),
                by_image(128),
                lead((8, GRID)),
                by_image(2 * D),
                lead((EXPERTS, GRID)),
            ],
            out_specs=[by_image(D), by_image(D), whole((D, DENSE)), whole((8, D))],
            scratch_shapes=[
                pltpu.VMEM((GRID, 3 * D), BF16),
                pltpu.VMEM((GRID, D), BF16),
                pltpu.VMEM((GRID, 128), F32),
                pltpu.VMEM((GRID, 128), F32),
                pltpu.VMEM((128, GRID), F32),
            ],
        ),
        out_shape=[
            jax.ShapeDtypeStruct((rows, D), BF16),
            jax.ShapeDtypeStruct((rows, D), BF16),
            jax.ShapeDtypeStruct((D, DENSE), F32),
            jax.ShapeDtypeStruct((8, D), F32),
        ],
        compiler_params=pltpu.CompilerParams(vmem_limit_bytes=VMEM_LIMIT),
        name="attention_backward",
    )(task_ids, tokens, cotangent, valid, dense, mixed, attended, resid, normed_b, aux, lse, sums, dprobs)


def body(
    tokens,
    cotangent,
    valid,
    task_ids,
    top_counts,
    expert_ids,
    attn_gain,
    attn_shift,
    proj_in,
    proj_out,
    moe_gain,
    moe_shift,
    router,
    expert_in,
    expert_out,
):
    own = attn_gain.shape[0]
    misc = jnp.concatenate(
        [
            jnp.stack([attn_gain, attn_shift, moe_gain, moe_shift], axis=1),
            router[0],
            router[1],
            jnp.zeros((own, 128 - 4 - TASKS * EXPERTS), BF16),
        ],
        axis=1,
    )
    packed = jnp.concatenate([proj_in, proj_out, misc], axis=1)
    dense = lax.all_gather(packed, "wide", axis=0, tiled=True)
    full_in = lax.all_gather(expert_in, "wide", axis=1, tiled=True)
    full_out = lax.all_gather(expert_out, "wide", axis=1, tiled=True)
    mixed, attended, resid, normed_b, aux, rows, lse = forward_call(
        task_ids, top_counts, tokens, valid, expert_ids, dense
    )
    sums, dprobs, grad_in, grad_out = expert_call(normed_b, cotangent, aux, rows, full_in, full_out)
    part_in = lax.psum_scatter(grad_in, "wide", scatter_dimension=1, tiled=True)
    part_out = lax.psum_scatter(grad_out, "wide", scatter_dimension=1, tiled=True)
    output, grad_tokens, grad_dense, _ = backward_call(
        task_ids, tokens, cotangent, valid, dense, mixed, attended, resid, normed_b, aux, lse, sums, dprobs
    )
    part_dense = lax.psum_scatter(grad_dense.astype(BF16), "wide", scatter_dimension=0, tiled=True)
    sum_in, sum_out, sum_dense = lax.psum((part_in, part_out, part_dense), "narrow")
    sum_in = sum_in.astype(F32)
    sum_out = sum_out.astype(F32)
    sum_dense = sum_dense.astype(F32)
    vectors = sum_dense[:, MISC : MISC + 4].T
    grad_router = jnp.stack(
        [sum_dense[:, MISC + 4 : MISC + 12], sum_dense[:, MISC + 12 : MISC + 20]], axis=0
    )
    return (
        output,
        grad_tokens,
        vectors[0],
        vectors[1],
        sum_dense[:, : 3 * D],
        sum_dense[:, 3 * D : MISC],
        vectors[2],
        vectors[3],
        grad_router,
        sum_in,
        sum_out,
    )


def solution(mesh):
    rows = P(("narrow", "wide"), None)
    middle = P(None, "wide", None)
    return jax.shard_map(
        body,
        mesh=mesh,
        in_specs=(
            rows,
            rows,
            rows,
            P(("narrow", "wide")),
            P(),
            rows,
            P("wide"),
            P("wide"),
            P("wide", None),
            P("wide", None),
            P("wide"),
            P("wide"),
            middle,
            middle,
            middle,
        ),
        out_specs=(
            rows,
            rows,
            P("wide"),
            P("wide"),
            P("wide", None),
            P("wide", None),
            P("wide"),
            P("wide"),
            middle,
            middle,
            middle,
        ),
        check_vma=False,
    )
```

time: 1290 us -> 653 us (0.51)
  matrix products: 278 us -> 0 us
  local copies, waits for them, and re-layouts: 269 us -> 22.2 us
  Pallas kernels: 0 us -> 182 us
  blocking collectives: 166 us -> 0 us
  other arithmetic: 114 us -> 7.77 us
  waiting for transfers between devices: 441 us -> 426 us
    dot_general x58 -> x0, matrix products: 278 us -> none  [the longest x2 35.1 us: experts_back(): jnp.einsum('ecd,efd->ecf', dresult, expert_pair[1], preferred_element_typ...]
    reduce_scatter x2 -> x1, waiting for transfers between devices: 389 us -> 115 us  [body(): lax.psum_scatter(grad_out, 'wide', scatter_dimension=1, tiled=True)]
    pallas_call x0 -> x3, Pallas kernels: none -> 182 us  [the longest x1 75 us: expert_call(): pl.pallas_call(functools.partial(expert_kernel, images), grid=(EXPERTS,),...]
    all_gather x2 -> x3, waiting for transfers between devices: 0.01 us -> 153 us  [the longest x1 81.9 us: body(): full_out = lax.all_gather(expert_out, 'wide', axis=1, tiled=True)]
    gather x12 -> x0, local copies, waits for them, and re-layouts: 141 us -> none  [the longest x4 48 us: backward_micro(): dnormed_b = jnp.sum(ddispatched[position], axis=1)]
    unnamed x9, waiting for transfers between devices: 1.48 us -> 110 us
    unnamed x2 -> x0, blocking collectives: 95.4 us -> none
    reduce_sum x23 -> x0, other arithmetic: 62.4 us -> none  [the longest x2 29.3 us: backward_micro(): dgates = jnp.sum(upstream[:, None, :] * picked, axis=-1) * kept_mask]
  transfers between devices with their start and end apart: 7 -> 7, of which waited for: 3 -> 7; matrix products, arithmetic and copies ran while one was open for 21% -> 1% of each run, Pallas kernels for 0% -> 16%
where the time goes in v1:
time: 653 us; the launch traced here: 652 us
  waiting for transfers between devices  426 us (65%)
  Pallas kernels  182 us (28%)
  local copies, waits for them, and re-layouts  22.2 us (3%)
  between operations  14.2 us (2%)
  other arithmetic  7.77 us (1%)
    reduce_scatter x1, waiting for transfers between devices, body(): lax.psum_scatter(grad_out, 'wide', scatter_dimension=1, tiled=True)  115 us
    unnamed x9, waiting for transfers between devices  110 us
    all_gather x1, waiting for transfers between devices, body(): full_out = lax.all_gather(expert_out, 'wide', axis=1, tiled=True)  81.9 us
    pallas_call x1, Pallas kernels, expert_call(): pl.pallas_call(functools.partial(expert_kernel, images), grid=(EXPERTS,),...  75 us
    pallas_call x1, Pallas kernels, backward_call(): pl.pallas_call(backward_kernel, grid_spec=pltpu.PrefetchScalarGridSpec(nu...  57.4 us
    pallas_call x1, Pallas kernels, forward_call(): pl.pallas_call(forward_kernel, grid_spec=pltpu.PrefetchScalarGridSpec(num...  49.4 us
    psum x1, waiting for transfers between devices, body(): lax.psum((part_in, part_out, part_dense), 'narrow')  47.8 us
    all_gather x1, waiting for transfers between devices, body(): dense = lax.all_gather(packed, 'wide', axis=0, tiled=True)  37.9 us
  transfers between devices with their start and end apart: 7, of which 7 were waited for; matrix products, arithmetic and copies ran while one was open for 1% of the time, Pallas kernels for 16%

profile of v1, /device:TPU:0, one launch (start us, length us, event | category | flops | bytes accessed | tf_op | source)
XLA Modules:
  0.0 652.0 jit_solution(15617987871266296357)
XLA Ops:
  7.2 0.0 all-gather.4.cloned.1.call-start
  7.2 0.7 fusion
  7.9 0.1 copy.54
  8.0 0.1 copy.53
  8.1 0.7 copy.44
  8.8 0.7 copy.45
  9.6 0.7 copy.46
  10.3 0.7 copy.47
  11.1 1.5 concatenate.3
  12.6 0.0 all-gather.4.cloned.1.call-update
  12.7 0.0 all-gather.6.cloned.1.call-start
  12.7 0.7 all-gather.6.cloned.1.call-update
  13.4 0.0 all-gather.8.cloned.1.call-start
  13.5 0.7 all-gather.8.cloned.1.call-update
  14.1 0.0 reduce-scatter.10.cloned.1.call-start
  14.2 2.1 copy.48.ids_ref
  16.3 37.9 %all-gather.4.cloned.1.call-done.dense_ref = bf16[384,1664]{1,0:T(8,128)(2,1)} async-done(((bf16[24,1664]{1,0:T(8,128)(2,1)}), bf16[384,1664]{1,0:T(8,128)(2,1)}) %all-gather.4.cloned.1.call-update) | async-done | bytes 1277968 | tf_op jit(solution)/shard_map/all_gather | solution.py:563
  54.2 49.4 %attention_forward.1 = (bf16[2048,1152]{1,0:T(8,128)(2,1)}, bf16[2048,384]{1,0:T(8,128)(2,1)}, f32[2048,384]{1,0:T(8,128)}, bf16[2048,384]{1,0:T(8,128)(2,1)}, f...) custom-call(s32[2]{0:T(128)} %task_ref.3, s32[2]{0:T(128)} %count_ref.1, ...), custom_call_target="tpu_custom_call" | custom-call | tf_op jit(solution)/shard_map/attention_forward/pallas_call | solution.py:186
  103.5 33.4 %all-gather.6.cloned.1.call-done.in_ref = bf16[8,384,1536]{2,1,0:T(8,128)(2,1)} async-done(((bf16[8,24,1536]{2,1,0:T(8,128)(2,1)}), bf16[8,384,1536]{2,1,0:T(8,128)(2,1)}) %all-gather.6.cloned.1.call-update) | async-done | bytes 9437200 | tf_op jit(solution)/shard_map/all_gather | solution.py:564
  136.9 81.9 %all-gather.8.cloned.1.call-done.out_ref = bf16[8,1536,384]{2,1,0:T(8,128)(2,1)} async-done(((bf16[8,96,384]{2,1,0:T(8,128)(2,1)}), bf16[8,1536,384]{2,1,0:T(8,128)(2,1)}) %all-gather.8.cloned.1.call-update) | async-done | bytes 9437200 | tf_op jit(solution)/shard_map/all_gather | solution.py:565
  218.8 75.0 %experts.1 = (f32[2048,768]{1,0:T(8,128)}, f32[2,8,1024]{2,1,0:T(8,128)}, bf16[8,384,1536]{2,1,0:T(8,128)(2,1)}, bf16[8,1536,384]{2,1,0:T(8,128)(2,1)}) custom-call(bf16[2048,384]{1,0:T(8,128)(2,1)} %get-tuple-element.28.normed_ref, bf16[2048,384]{1,0:T(8,128)(2,1)} %cot_ref.3, f32[2048,128]{1,0:T(8,128)} %get-tuple-element.29.aux_ref, ...), custom_call_target="tpu_custom_call" | custom-call | tf_op jit(solution)/shard_map/experts/pallas_call | solution.py:304
  293.8 8.7 %copy.55 = bf16[48,8,8,1536]{3,1,2,0:T(8,128)(2,1)} copy(bf16[48,8,8,1536]{3,1,0,2:T(8,128)(2,1)} %bitcast.22) | data formatting | bytes 18874368
  302.5 0.0 reduce-scatter.10.cloned.1.call-update
  302.5 0.0 reduce-scatter.12.cloned.1.call-start
  302.6 57.4 %attention_backward.1 = (bf16[2048,384]{1,0:T(8,128)(2,1)}, bf16[2048,384]{1,0:T(8,128)(2,1)}, f32[384,1664]{1,0:T(8,128)}, f32[8,384]{1,0:T(8,128)}) custom-call(s32[2]{0:T(128)} %task_ref.3, bf16[2048,384]{1,0:T(8,128)(2,1)} %tokens_ref.3, bf16[2048,384]{1,0:T(8,128)(2,1)} %cot_ref.3, s32[2,1024]{1,0:T(2,128)} %valid_ref.3, ...), custom_call_target="tpu_custom_call" | custom-call | tf_op jit(solution)/shard_map/attention_backward/pallas_call | solution.py:496
  360.0 3.0 convert_element_type.12
  362.9 0.0 reduce-scatter.12.cloned.1.call-update
  363.0 0.0 reduce-scatter.8.cloned.1.call-start
  363.0 0.5 reduce-scatter.8.cloned.1.call-update
  363.5 0.0 all-reduce.4.cloned.1.call-start
  363.6 48.6 %reduce-scatter.10.cloned.1.call-done = bf16[24,12288]{1,0:T(8,128)(2,1)} async-done(((bf16[384,12288]{1,0:T(8,128)(2,1)}), bf16[24,12288]{1,0:T(8,128)(2,1)}) %reduce-scatter.10.cloned.1.call-update) | async-done | bytes 589840
  412.2 1.2 copy.56
  413.4 1.0 copy.52
  414.4 59.3 %reduce-scatter.12.cloned.1.call-done = bf16[24,1664]{1,0:T(8,128)(2,1)} async-done(((bf16[384,1664]{1,0:T(8,128)(2,1)}), bf16[24,1664]{1,0:T(8,128)(2,1)}) %reduce-scatter.12.cloned.1.call-update) | async-done | bytes 79888
  473.8 114.9 %reduce-scatter.8.cloned.1.call-done = bf16[8,96,384]{2,1,0:T(8,128)(2,1)} async-done(((bf16[8,1536,384]{2,1,0:T(8,128)(2,1)}), bf16[8,96,384]{2,1,0:T(8,128)(2,1)}) %reduce-scatter.8.cloned.1.call-update) | async-done | bytes 589840 | tf_op jit(solution)/shard_map/reduce_scatter | solution.py:571
  588.6 0.0 all-reduce.4.cloned.1.call-update
  588.7 47.8 %all-reduce.4.cloned.1.call-done = (bf16[24,1664]{1,0:T(8,128)(2,1)}, bf16[8,24,1536]{2,1,0:T(8,128)(2,1)}, bf16[8,96,384]{2,1,0:T(8,128)(2,1)}) async-done(((bf16[24,1664]{1,0:T(8,128)(2,1)}, bf16[8,24,1536]{2,1,0:T(8,128)(2,1)}, bf16[8,96,384]{2,1,0:T(8,128)(2,1)}), (bf16[24,1664]{1,0:T(8,128)(2,1)}, bf16[8,24,1536]{2,1,0:T(8,128)(2,1)}, bf16[8,96,384]{2,1,0:T(8,128)(2,1)})) %all-reduce.4.cloned.1.call-update) | async-done | bytes 1259536 | tf_op jit(solution)/shard_map/psum | solution.py:576
  636.5 1.4 slice.48
  637.9 1.5 slice.47
  639.4 0.9 convert_element_type.13
  640.3 0.1 slice_bitcast_fusion.1
  640.4 0.7 slice_reduce_fusion
  641.1 0.1 copy.49
  641.2 0.1 copy.50
  641.2 2.2 convert_element_type.14
  643.5 0.0 copy-done
  643.5 1.1 convert_element_type.15
  644.5 0.6 pad_maximum_fusion
  (3 shorter events, 0.0 us)
Async XLA Ops:
  7.2 47.0 %all-gather.4.cloned.1.call-start = ((), (), s32[]{:S(2)}) async-start(), calls=%async_computation.3 | async-start | bytes 1357824 | tf_op jit(solution)/shard_map/all_gather | solution.py:563
  12.7 124.2 %all-gather.6.cloned.1.call-start = ((), (), s32[]{:S(2)}) async-start(), calls=%async_computation.4 | async-start | bytes 10027008 | tf_op jit(solution)/shard_map/all_gather | solution.py:564
  13.4 205.4 %all-gather.8.cloned.1.call-start = ((), (), s32[]{:S(2)}) async-start(), calls=%async_computation.5 | async-start | bytes 10027008 | tf_op jit(solution)/shard_map/all_gather | solution.py:565
  14.1 398.0 %reduce-scatter.10.cloned.1.call-start = ((), (), s32[]{:S(2)}) async-start(), calls=%async_computation.7 | async-start | bytes 10027008
  302.5 171.2 %reduce-scatter.12.cloned.1.call-start = ((), (), s32[]{:S(2)}) async-start(), calls=%async_computation.8 | async-start | bytes 1357824
  363.0 225.7 %reduce-scatter.8.cloned.1.call-start = ((), (), s32[]{:S(2)}) async-start(), calls=%async_computation.6 | async-start | bytes 10027008 | tf_op jit(solution)/shard_map/reduce_scatter | solution.py:571
  363.5 273.0 %all-reduce.4.cloned.1.call-start = ((), (), s32[]{:S(2)}) async-start(), calls=%async_computation.9 | async-start | bytes 2519040 | tf_op jit(solution)/shard_map/psum | solution.py:576
  636.5 6.9 %copy-start = (bf16[8,96,384]{2,1,0:T(8,128)(2,1)S(1)}, bf16[8,96,384]{2,1,0:T(8,128)(2,1)}, u32[]{:S(2)}) copy-start(bf16[8,96,384]{2,1,0:T(8,128)(2,1)} %get-tuple-element.67) | copy-start | bytes 1769476
Sparse Core Ops, SparseCore 0:
  12.8 41.3 all-gather.3
  56.4 80.4 all-gather.5
  139.2 79.5 all-gather.7
  302.7 109.4 reduce-scatter.9
  416.2 57.5 reduce-scatter.11
  478.3 110.3 reduce-scatter.7
  591.7 44.7 all-reduce.3

commit v2 on v1

--- a/solution.py
+++ b/solution.py
@@ -76,6 +76,32 @@
     return jnp.broadcast_to(row, (128, row.shape[1])).T
 
 
+MESH = pl.DeviceIdType.MESH
+
+
+def hello(first, last, here, there, sems):
+    def copy():
+        core = lax.axis_index("wide") ^ 1
+        return pltpu.make_async_remote_copy(
+            src_ref=here, dst_ref=there, send_sem=sems.at[0], recv_sem=sems.at[1],
+            device_id={"wide": core}, device_id_type=MESH)
+
+    @pl.when(first)
+    def _():
+        barrier = pltpu.get_barrier_semaphore()
+        pl.semaphore_signal(barrier, inc=1, device_id={"wide": lax.axis_index("wide") ^ 1}, device_id_type=MESH)
+        pl.semaphore_wait(barrier, 1)
+        here[...] = jnp.ones_like(here)
+        copy().start()
+
+    @pl.when(last)
+    def _():
+        copy().wait()
+
+
+HELLO = [pltpu.VMEM((16, 128), jnp.bfloat16), pltpu.VMEM((16, 128), jnp.bfloat16), pltpu.SemaphoreType.DMA((2,))]
+
+
 def forward_kernel(
     task_ref,
     count_ref,
@@ -91,7 +117,9 @@
     rows_ref,
     lse_ref,
     att_t,
+    *more,
 ):
+    hello(pl.program_id(0) == 0, pl.program_id(0) == pl.num_programs(0) - 1, *more)
     image = pl.program_id(0)
     task = task_ref[image]
     count = count_ref[task]
@@ -180,15 +208,16 @@
 def forward_call(task_ids, top_counts, tokens, valid, expert_ids, dense):
     images = valid.shape[0]
     rows = images * GRID
+    smem = pl.BlockSpec(memory_space=pltpu.SMEM)
     by_image = lambda width: pl.BlockSpec((GRID, width), lambda i, *_: (i, 0))
     whole = lambda shape: pl.BlockSpec(shape, lambda i, *_: (0,) * len(shape))
     lead = lambda shape: pl.BlockSpec((1,) + shape, lambda i, *_: (i, 0, 0))
     return pl.pallas_call(
         forward_kernel,
         grid_spec=pltpu.PrefetchScalarGridSpec(
-            num_scalar_prefetch=2,
+            num_scalar_prefetch=0,
             grid=(images,),
-            in_specs=[by_image(D), whole(valid.shape), by_image(TOPMAX), whole(dense.shape)],
+            in_specs=[smem, smem, by_image(D), whole(valid.shape), by_image(TOPMAX), whole(dense.shape)],
             out_specs=[
                 by_image(3 * D),
                 by_image(D),
@@ -198,7 +227,7 @@
                 lead((4 * EXPERTS, GRID)),
                 lead((8, GRID)),
             ],
-            scratch_shapes=[pltpu.VMEM((D, GRID), F32)],
+            scratch_shapes=[pltpu.VMEM((D, GRID), F32)] + HELLO,
         ),
         out_shape=[
             jax.ShapeDtypeStruct((rows, 3 * D), BF16),
@@ -209,7 +238,7 @@
             jax.ShapeDtypeStruct((images, 4 * EXPERTS, GRID), F32),
             jax.ShapeDtypeStruct((images, 8, GRID), F32),
         ],
-        compiler_params=pltpu.CompilerParams(vmem_limit_bytes=VMEM_LIMIT),
+        compiler_params=pltpu.CompilerParams(vmem_limit_bytes=VMEM_LIMIT, collective_id=0, has_side_effects=True),
         name="attention_forward",
     )(task_ids, top_counts, tokens, valid, expert_ids, dense)
 
@@ -230,7 +259,9 @@
     given,
     upstream,
     dres_s,
+    *more,
 ):
+    hello(pl.program_id(0) == 0, pl.program_id(0) == pl.num_programs(0) - 1, *more)
     expert = pl.program_id(0)
 
     @pl.when(expert == 0)
@@ -329,8 +360,8 @@
             pltpu.VMEM((images * CAP, D), BF16),
             pltpu.VMEM((images * CAP, D + 128), F32),
             pltpu.VMEM((images * CAP, D), BF16),
-        ],
-        compiler_params=pltpu.CompilerParams(vmem_limit_bytes=VMEM_LIMIT),
+        ] + HELLO,
+        compiler_params=pltpu.CompilerParams(vmem_limit_bytes=VMEM_LIMIT, collective_id=1, has_side_effects=True),
         name="experts",
     )(normed_b, cotangent, aux, rows, expert_in, expert_out)
 
@@ -365,7 +396,9 @@
     acc_k,
     acc_v,
     dq_t,
+    *more,
 ):
+    hello(pl.program_id(0) == 0, pl.program_id(0) == pl.num_programs(0) - 1, *more)
     image = pl.program_id(0)
     task = task_ref[image]
     misc = misc_rows(dense_ref)
@@ -490,15 +523,17 @@
 ):
     images = valid.shape[0]
     rows = images * GRID
+    smem = pl.BlockSpec(memory_space=pltpu.SMEM)
     by_image = lambda width: pl.BlockSpec((GRID, width), lambda i, *_: (i, 0))
     whole = lambda shape: pl.BlockSpec(shape, lambda i, *_: (0,) * len(shape))
     lead = lambda shape: pl.BlockSpec((1,) + shape, lambda i, *_: (i, 0, 0))
     return pl.pallas_call(
         backward_kernel,
         grid_spec=pltpu.PrefetchScalarGridSpec(
-            num_scalar_prefetch=1,
+            num_scalar_prefetch=0,
             grid=(images,),
             in_specs=[
+                smem,
                 by_image(D),
                 by_image(D),
                 whole(valid.shape),
@@ -519,7 +554,7 @@
                 pltpu.VMEM((GRID, 128), F32),
                 pltpu.VMEM((GRID, 128), F32),
                 pltpu.VMEM((128, GRID), F32),
-            ],
+            ] + HELLO,
         ),
         out_shape=[
             jax.ShapeDtypeStruct((rows, D), BF16),
@@ -527,7 +562,7 @@
             jax.ShapeDtypeStruct((D, DENSE), F32),
             jax.ShapeDtypeStruct((8, D), F32),
         ],
-        compiler_params=pltpu.CompilerParams(vmem_limit_bytes=VMEM_LIMIT),
+        compiler_params=pltpu.CompilerParams(vmem_limit_bytes=VMEM_LIMIT, collective_id=2, has_side_effects=True),
         name="attention_backward",
     )(task_ids, tokens, cotangent, valid, dense, mixed, attended, resid, normed_b, aux, lse, sums, dprobs)
 

time: 653 us -> 657 us (level)
    unnamed x8 -> x14, local copies, waits for them, and re-layouts: 13.2 us -> 16.3 us
where the time goes in v2:
time: 657 us; the launch traced here: 656 us
  waiting for transfers between devices  428 us (65%)
  Pallas kernels  181 us (28%)
  local copies, waits for them, and re-layouts  25.4 us (4%)
  between operations  14.2 us (2%)
  other arithmetic  7.9 us (1%)
    reduce_scatter x1, waiting for transfers between devices, body(): lax.psum_scatter(grad_out, 'wide', scatter_dimension=1, tiled=True)  115 us
    unnamed x9, waiting for transfers between devices  111 us
    all_gather x1, waiting for transfers between devices, body(): full_out = lax.all_gather(expert_out, 'wide', axis=1, tiled=True)  81.9 us
    pallas_call x1, Pallas kernels, expert_call(): pl.pallas_call(functools.partial(expert_kernel, images), grid=(EXPERTS,),...  75.3 us
    pallas_call x1, Pallas kernels, backward_call(): pl.pallas_call(backward_kernel, grid_spec=pltpu.PrefetchScalarGridSpec(nu...  56.8 us
    pallas_call x1, Pallas kernels, forward_call(): pl.pallas_call(forward_kernel, grid_spec=pltpu.PrefetchScalarGridSpec(num...  48.6 us
    psum x1, waiting for transfers between devices, body(): lax.psum((part_in, part_out, part_dense), 'narrow')  47.8 us
    all_gather x1, waiting for transfers between devices, body(): dense = lax.all_gather(packed, 'wide', axis=0, tiled=True)  37.9 us
  transfers between devices with their start and end apart: 7, of which 7 were waited for; matrix products, arithmetic and copies ran while one was open for 1% of the time, Pallas kernels for 16%

profile of v2, /device:TPU:0, one launch (start us, length us, event | category | flops | bytes accessed | tf_op | source)
XLA Modules:
  0.0 656.2 jit_solution(9035604511454536372)
XLA Ops:
  7.2 0.0 all-gather.4.cloned.1.call-start
  7.2 0.7 fusion
  7.9 0.1 copy.54
  8.0 0.1 copy.53
  8.1 0.7 copy.44
  8.8 0.7 copy.45
  9.6 0.7 copy.46
  10.3 0.7 copy.47
  11.1 1.5 concatenate.3
  12.7 0.0 all-gather.6.cloned.1.call-start
  12.7 0.7 all-gather.6.cloned.1.call-update
  13.4 0.0 all-gather.8.cloned.1.call-start
  13.5 0.7 all-gather.8.cloned.1.call-update
  14.1 0.0 reduce-scatter.10.cloned.1.call-start
  14.2 2.1 copy.48.ids_ref
  16.3 37.9 %all-gather.4.cloned.1.call-done.dense_ref = bf16[384,1664]{1,0:T(8,128)(2,1)} async-done(((bf16[24,1664]{1,0:T(8,128)(2,1)}), bf16[384,1664]{1,0:T(8,128)(2,1)}) %all-gather.4.cloned.1.call-update) | async-done | bytes 1277968 | tf_op jit(solution)/shard_map/all_gather | solution.py:598
  54.2 48.6 %attention_forward.1 = (bf16[2048,1152]{1,0:T(8,128)(2,1)}, bf16[2048,384]{1,0:T(8,128)(2,1)}, f32[2048,384]{1,0:T(8,128)}, bf16[2048,384]{1,0:T(8,128)(2,1)}, f...) custom-call(s32[2]{0:T(128)} %task_ref.3, s32[2]{0:T(128)} %count_ref.1, ...), custom_call_target="tpu_custom_call" | custom-call | tf_op jit(solution)/shard_map/attention_forward/pallas_call | solution.py:215
  102.8 34.1 %all-gather.6.cloned.1.call-done.in_ref = bf16[8,384,1536]{2,1,0:T(8,128)(2,1)} async-done(((bf16[8,24,1536]{2,1,0:T(8,128)(2,1)}), bf16[8,384,1536]{2,1,0:T(8,128)(2,1)}) %all-gather.6.cloned.1.call-update) | async-done | bytes 9437200 | tf_op jit(solution)/shard_map/all_gather | solution.py:599
  136.9 81.9 %all-gather.8.cloned.1.call-done.out_ref = bf16[8,1536,384]{2,1,0:T(8,128)(2,1)} async-done(((bf16[8,96,384]{2,1,0:T(8,128)(2,1)}), bf16[8,1536,384]{2,1,0:T(8,128)(2,1)}) %all-gather.8.cloned.1.call-update) | async-done | bytes 9437200 | tf_op jit(solution)/shard_map/all_gather | solution.py:600
  218.8 75.3 %experts.1 = (f32[2048,768]{1,0:T(8,128)}, f32[2,8,1024]{2,1,0:T(8,128)}, bf16[8,384,1536]{2,1,0:T(8,128)(2,1)}, bf16[8,1536,384]{2,1,0:T(8,128)(2,1)}) custom-call(bf16[2048,384]{1,0:T(8,128)(2,1)} %get-tuple-element.28.normed_ref, bf16[2048,384]{1,0:T(8,128)(2,1)} %cot_ref.3, f32[2048,128]{1,0:T(8,128)} %get-tuple-element.29.aux_ref, ...), custom_call_target="tpu_custom_call" | custom-call | tf_op jit(solution)/shard_map/experts/pallas_call | solution.py:335
  294.2 8.7 %copy.55 = bf16[48,8,8,1536]{3,1,2,0:T(8,128)(2,1)} copy(bf16[48,8,8,1536]{3,1,0,2:T(8,128)(2,1)} %bitcast.22) | data formatting | bytes 18874368
  302.9 0.0 reduce-scatter.10.cloned.1.call-update
  302.9 0.0 reduce-scatter.12.cloned.1.call-start
  302.9 56.8 %attention_backward.1 = (bf16[2048,384]{1,0:T(8,128)(2,1)}, bf16[2048,384]{1,0:T(8,128)(2,1)}, f32[384,1664]{1,0:T(8,128)}, f32[8,384]{1,0:T(8,128)}) custom-call(s32[2]{0:T(128)} %task_ref.3, bf16[2048,384]{1,0:T(8,128)(2,1)} %tokens_ref.3, bf16[2048,384]{1,0:T(8,128)(2,1)} %cot_ref.3, s32[2,1024]{1,0:T(2,128)} %valid_ref.3, ...), custom_call_target="tpu_custom_call" | custom-call | tf_op jit(solution)/shard_map/attention_backward/pallas_call | solution.py:530
  359.7 3.0 convert_element_type.12
  362.7 0.0 reduce-scatter.12.cloned.1.call-update
  362.7 0.0 reduce-scatter.8.cloned.1.call-start
  362.7 0.5 reduce-scatter.8.cloned.1.call-update
  363.3 0.0 all-reduce.4.cloned.1.call-start
  363.3 49.2 %reduce-scatter.10.cloned.1.call-done = bf16[24,12288]{1,0:T(8,128)(2,1)} async-done(((bf16[384,12288]{1,0:T(8,128)(2,1)}), bf16[24,12288]{1,0:T(8,128)(2,1)}) %reduce-scatter.10.cloned.1.call-update) | async-done | bytes 589840
  412.6 1.2 copy.56
  413.8 1.0 copy.52
  414.8 59.9 %reduce-scatter.12.cloned.1.call-done = bf16[24,1664]{1,0:T(8,128)(2,1)} async-done(((bf16[384,1664]{1,0:T(8,128)(2,1)}), bf16[24,1664]{1,0:T(8,128)(2,1)}) %reduce-scatter.12.cloned.1.call-update) | async-done | bytes 79888
  474.7 114.9 %reduce-scatter.8.cloned.1.call-done = bf16[8,96,384]{2,1,0:T(8,128)(2,1)} async-done(((bf16[8,1536,384]{2,1,0:T(8,128)(2,1)}), bf16[8,96,384]{2,1,0:T(8,128)(2,1)}) %reduce-scatter.8.cloned.1.call-update) | async-done | bytes 589840 | tf_op jit(solution)/shard_map/reduce_scatter | solution.py:606
  589.6 47.8 %all-reduce.4.cloned.1.call-done = (bf16[24,1664]{1,0:T(8,128)(2,1)}, bf16[8,24,1536]{2,1,0:T(8,128)(2,1)}, bf16[8,96,384]{2,1,0:T(8,128)(2,1)}) async-done(((bf16[24,1664]{1,0:T(8,128)(2,1)}, bf16[8,24,1536]{2,1,0:T(8,128)(2,1)}, bf16[8,96,384]{2,1,0:T(8,128)(2,1)}), (bf16[24,1664]{1,0:T(8,128)(2,1)}, bf16[8,24,1536]{2,1,0:T(8,128)(2,1)}, bf16[8,96,384]{2,1,0:T(8,128)(2,1)})) %all-reduce.4.cloned.1.call-update) | async-done | bytes 1259536 | tf_op jit(solution)/shard_map/psum | solution.py:611
  637.5 1.4 slice.48
  638.9 1.5 slice.47
  640.4 0.9 convert_element_type.13
  641.3 0.1 slice_bitcast_fusion.1
  641.4 0.7 slice_reduce_fusion
  642.1 0.1 copy.49
  642.2 0.1 copy.50
  642.2 2.3 convert_element_type.14
  644.6 1.1 convert_element_type.15
  645.7 0.6 pad_maximum_fusion
  646.3 1.1 copy.63
  647.4 0.8 copy-done
  648.2 1.1 copy.64
  (9 shorter events, 0.0 us)
Async XLA Ops:
  7.2 47.0 %all-gather.4.cloned.1.call-start = ((), (), s32[]{:S(2)}) async-start(), calls=%async_computation.3 | async-start | bytes 1357824 | tf_op jit(solution)/shard_map/all_gather | solution.py:598
  12.7 124.3 %all-gather.6.cloned.1.call-start = ((), (), s32[]{:S(2)}) async-start(), calls=%async_computation.4 | async-start | bytes 10027008 | tf_op jit(solution)/shard_map/all_gather | solution.py:599
  13.4 205.4 %all-gather.8.cloned.1.call-start = ((), (), s32[]{:S(2)}) async-start(), calls=%async_computation.5 | async-start | bytes 10027008 | tf_op jit(solution)/shard_map/all_gather | solution.py:600
  14.1 398.4 %reduce-scatter.10.cloned.1.call-start = ((), (), s32[]{:S(2)}) async-start(), calls=%async_computation.7 | async-start | bytes 10027008
  302.9 171.9 %reduce-scatter.12.cloned.1.call-start = ((), (), s32[]{:S(2)}) async-start(), calls=%async_computation.8 | async-start | bytes 1357824
  362.7 226.9 %reduce-scatter.8.cloned.1.call-start = ((), (), s32[]{:S(2)}) async-start(), calls=%async_computation.6 | async-start | bytes 10027008 | tf_op jit(solution)/shard_map/reduce_scatter | solution.py:606
  363.3 274.2 %all-reduce.4.cloned.1.call-start = ((), (), s32[]{:S(2)}) async-start(), calls=%async_computation.9 | async-start | bytes 2519040 | tf_op jit(solution)/shard_map/psum | solution.py:611
  637.5 7.1 %copy-start.2 = (bf16[8,96,384]{2,1,0:T(8,128)(2,1)S(1)}, bf16[8,96,384]{2,1,0:T(8,128)(2,1)}, u32[]{:S(2)}) copy-start(bf16[8,96,384]{2,1,0:T(8,128)(2,1)} %get-tuple-element.67) | copy-start | bytes 1769476
  642.2 4.0 copy-start.1
  646.3 2.0 copy-start
Sparse Core Ops, SparseCore 0:
  12.8 41.3 all-gather.3
  56.4 80.4 all-gather.5
  139.2 79.5 all-gather.7
  303.0 109.5 reduce-scatter.9
  417.2 57.5 reduce-scatter.11
  479.2 110.3 reduce-scatter.7
  592.7 44.7 all-reduce.3

commit v3 on v1

--- a/solution.py
+++ b/solution.py
@@ -530,6 +530,918 @@
         compiler_params=pltpu.CompilerParams(vmem_limit_bytes=VMEM_LIMIT),
         name="attention_backward",
     )(task_ids, tokens, cotangent, valid, dense, mixed, attended, resid, normed_b, aux, lse, sums, dprobs)
+
+
+MESH = pl.DeviceIdType.MESH
+ZS = 4
+XS = 2
+CORES = 2
+HALF_ROWS = 48
+WIDE_LANES = 768
+DENSE_LANES = 512
+DENSE_COLS = 2048
+FCH = 768
+
+
+class Place:
+    def __init__(self):
+        self.w = lax.axis_index("wide")
+        self.y = lax.axis_index("narrow")
+        self.c = lax.rem(self.w, CORES)
+        self.x = lax.rem(self.w // CORES, XS)
+        self.z = self.w // (CORES * XS)
+
+    def wide(self, z, x, c):
+        return (z * XS + x) * CORES + c
+
+    def core_peer(self):
+        return {"wide": self.wide(self.z, self.x, 1 - self.c)}
+
+    def x_peer(self):
+        return {"wide": self.wide(self.z, 1 - self.x, self.c)}
+
+    def y_peer(self):
+        return {"narrow": 1 - self.y}
+
+    def z_ahead(self, k):
+        return lax.rem(self.z + k, ZS)
+
+    def z_behind(self, k):
+        return lax.rem(self.z + ZS - k, ZS)
+
+    def z_peer(self, k):
+        return {"wide": self.wide(self.z_ahead(k), self.x, self.c)}
+
+
+def remote(src, dst, sems, to):
+    return pltpu.make_async_remote_copy(
+        src_ref=src, dst_ref=dst, send_sem=sems[0], recv_sem=sems[1], device_id=to, device_id_type=MESH
+    )
+
+
+class Gather:
+    def __init__(self, place, mine, wall, zs, zr, xs, xr, ys, yr, as_, ar, bs, br):
+        self.p = place
+        self.mine, self.wall = mine, wall
+        self.z_sem, self.x_sem, self.y_sem = (zs, zr), (xs, xr), (ys, yr)
+        self.a_sem, self.b_sem = (as_, ar), (bs, br)
+
+    def pair(self, sems, *at):
+        return sems[0].at[at], sems[1].at[at]
+
+    def z_copy(self, e, k):
+        p = self.p
+        return remote(self.mine.at[e], self.wall.at[e, p.x, p.c, p.z], self.pair(self.z_sem, e, k - 1), p.z_peer(k))
+
+    def z_landed(self, e, k):
+        p = self.p
+        here = self.wall.at[e, p.x, p.c, p.z_behind(k)]
+        return remote(here, here, self.pair(self.z_sem, e, k - 1), p.z_peer(k))
+
+    def x_copy(self, e, x):
+        p = self.p
+        here = self.wall.at[e, x, p.c, :, p.y]
+        return remote(here, here, self.pair(self.x_sem, e), p.x_peer())
+
+    def y_copy(self, e, y):
+        p = self.p
+        here = self.wall.at[e, 1 - p.x, p.c, :, y]
+        return remote(here, here, self.pair(self.y_sem, e), p.y_peer())
+
+    def a_copy(self, e, c):
+        p = self.p
+        here = self.wall.at[e, p.x, c]
+        return remote(here, here, self.pair(self.a_sem, e), p.core_peer())
+
+    def b_copy(self, e, c):
+        p = self.p
+        here = self.wall.at[e, 1 - p.x, c]
+        return remote(here, here, self.pair(self.b_sem, e), p.core_peer())
+
+    def t0(self, e):
+        for k in range(1, ZS):
+            self.z_copy(e, k).start()
+
+    def t1(self, e):
+        for k in range(1, ZS):
+            self.z_landed(e, k).wait_recv()
+        self.x_copy(e, self.p.x).start()
+        self.a_copy(e, self.p.c).start()
+
+    def t2(self, e):
+        self.x_copy(e, 1 - self.p.x).wait_recv()
+        self.y_copy(e, self.p.y).start()
+
+    def t3(self, e):
+        self.y_copy(e, 1 - self.p.y).wait_recv()
+        self.b_copy(e, self.p.c).start()
+
+    def t4(self, e):
+        self.a_copy(e, 1 - self.p.c).wait_recv()
+        self.b_copy(e, 1 - self.p.c).wait_recv()
+
+    def drain(self, e):
+        for k in range(1, ZS):
+            self.z_copy(e, k).wait_send()
+        self.x_copy(e, self.p.x).wait_send()
+        self.a_copy(e, self.p.c).wait_send()
+        self.y_copy(e, self.p.y).wait_send()
+        self.b_copy(e, self.p.c).wait_send()
+
+
+def add16(a, b):
+    return (a.astype(F32) + b.astype(F32)).astype(BF16)
+
+
+class Scatter:
+    def __init__(self, place, gs, rc, s1, rxa, ryb, s2a, s2b, rya, rxb, s3, rz, fb, send, land):
+        self.p = place
+        self.gs, self.rc, self.s1 = gs, rc, s1
+        self.rxa, self.ryb, self.s2a, self.s2b = rxa, ryb, s2a, s2b
+        self.rya, self.rxb, self.s3, self.rz, self.fb = rya, rxb, s3, rz, fb
+        self.send, self.land = send, land
+
+    def sems(self, which, slot):
+        return self.send.at[which, slot], self.land.at[which, slot]
+
+    def cut(self, ref, lanes_):
+        return ref.at[..., pl.ds(0, lanes_)] if lanes_ != WIDE_LANES else ref
+
+    def c_copy(self, slot, n):
+        p = self.p
+        return remote(
+            self.cut(self.gs.at[slot, 1 - p.c], n), self.cut(self.rc.at[slot], n), self.sems(0, slot), p.core_peer()
+        )
+
+    def xa_copy(self, slot, n):
+        p = self.p
+        return remote(
+            self.cut(self.s1.at[1 - p.x, pl.ds(0, 2)], n),
+            self.cut(self.rxa.at[slot], n),
+            self.sems(1, slot),
+            p.x_peer(),
+        )
+
+    def yb_copy(self, slot, n):
+        p = self.p
+        return remote(
+            self.cut(self.s1.at[:, pl.ds(2, 2), 1 - p.y], n),
+            self.cut(self.ryb.at[slot], n),
+            self.sems(2, slot),
+            p.y_peer(),
+        )
+
+    def ya_copy(self, slot, n):
+        p = self.p
+        return remote(
+            self.cut(self.s2a.at[:, 1 - p.y], n), self.cut(self.rya.at[slot], n), self.sems(3, slot), p.y_peer()
+        )
+
+    def xb_copy(self, slot, n):
+        p = self.p
+        return remote(
+            self.cut(self.s2b.at[1 - p.x], n), self.cut(self.rxb.at[slot], n), self.sems(4, slot), p.x_peer()
+        )
+
+    def z_copy(self, slot, k, n):
+        p = self.p
+        return remote(
+            self.cut(self.s3.at[p.z_ahead(k)], n),
+            self.cut(self.rz.at[slot, k - 1], n),
+            self.sems(4 + k, slot),
+            p.z_peer(k),
+        )
+
+    def f_copy(self, slot, y, n):
+        here = self.cut(self.fb.at[slot, y], n)
+        return remote(here, here, self.sems(8, slot), self.p.y_peer())
+
+    def r0(self, slot, n=WIDE_LANES):
+        self.c_copy(slot, n).start()
+
+    def r1(self, slot, n=WIDE_LANES):
+        p = self.p
+        self.c_copy(slot, n).wait()
+        for x in range(XS):
+            for z in range(ZS):
+                self.s1[x, z, :, :, :n] = add16(self.gs[slot, p.c, x, z, :, :, :n], self.rc[slot, x, z, :, :, :n])
+        self.xa_copy(slot, n).start()
+        self.yb_copy(slot, n).start()
+
+    def r2(self, slot, n=WIDE_LANES):
+        p = self.p
+        self.xa_copy(slot, n).wait()
+        self.yb_copy(slot, n).wait()
+        for z in range(2):
+            self.s2a[z, :, :, :n] = add16(self.s1[p.x, z, :, :, :n], self.rxa[slot, z, :, :, :n])
+            for x in range(XS):
+                self.s2b[x, z, :, :n] = add16(self.s1[x, 2 + z, p.y, :, :n], self.ryb[slot, x, z, :, :n])
+        self.ya_copy(slot, n).start()
+        self.xb_copy(slot, n).start()
+
+    def r3(self, slot, n=WIDE_LANES):
+        p = self.p
+        self.ya_copy(slot, n).wait()
+        self.xb_copy(slot, n).wait()
+        for z in range(2):
+            self.s3[z, :, :n] = add16(self.s2a[z, p.y, :, :n], self.rya[slot, z, :, :n])
+            self.s3[2 + z, :, :n] = add16(self.s2b[p.x, z, :, :n], self.rxb[slot, z, :, :n])
+        for k in range(1, ZS):
+            self.z_copy(slot, k, n).start()
+
+    def r4(self, slot, n=WIDE_LANES):
+        p = self.p
+        for k in range(1, ZS):
+            self.z_copy(slot, k, n).wait()
+        total = self.s3[p.z, :, :n].astype(F32)
+        for k in range(1, ZS):
+            total = total + self.rz[slot, k - 1, :, :n].astype(F32)
+        self.fb[slot, p.y, :, :n] = total.astype(BF16)
+        self.f_copy(slot, p.y, n).start()
+
+    def r5(self, slot, n=WIDE_LANES):
+        p = self.p
+        self.f_copy(slot, p.y, n).wait_send()
+        self.f_copy(slot, 1 - p.y, n).wait_recv()
+        return self.fb[slot, 0, :, :n].astype(F32), self.fb[slot, 1, :, :n].astype(F32)
+
+
+def routing(task, count, ids_ref, valid_ref, image, slots_ref):
+    at = pl.multiple_of(image * GRID, GRID)
+    live = valid_ref[pl.ds(image, 1), :] > 0
+    kind = lax.broadcasted_iota(jnp.int32, (EXPERTS, GRID), 0)
+    marks = []
+    for rank in range(TOPMAX):
+        hit = (ids_ref[pl.ds(rank, 1), pl.ds(at, GRID)] == kind) & live & (rank < count)
+        marks.append(jnp.where(hit, 1.0, 0.0))
+    used = jnp.concatenate(marks, axis=0)
+    span = 256
+    from_at = lax.broadcasted_iota(jnp.int32, (span, span), 0)
+    earlier = jnp.where(from_at < lanes((span, span)), 1.0, 0.0).astype(BF16)
+    running = jnp.zeros((TOPMAX * EXPERTS, 1), F32)
+    pieces = []
+    for block in range(GRID // span):
+        part = used[:, block * span : (block + 1) * span]
+        pieces.append(nn(part.astype(BF16), earlier) + running)
+        running = running + jnp.sum(part, axis=1, keepdims=True)
+    before = jnp.concatenate(pieces, axis=1)
+    found = jnp.zeros((EXPERTS, GRID), F32)
+    base = jnp.zeros((EXPERTS, 1), F32)
+    for rank in range(TOPMAX):
+        rows = slice(rank * EXPERTS, (rank + 1) * EXPERTS)
+        slot = before[rows] + base
+        found = found + jnp.where((used[rows] > 0.5) & (slot < CAP), slot + 1.0, 0.0)
+        base = base + running[rows]
+    slots_ref[image, :EXPERTS] = found - 1.0
+
+
+def whole_kernel(
+    images,
+    task_ref,
+    count_ref,
+    tokens_ref,
+    cot_ref,
+    valid_ref,
+    ids_ref,
+    dmine,
+    mine,
+    output_ref,
+    grad_tokens_ref,
+    grad_in_ref,
+    grad_out_ref,
+    grad_dense_ref,
+    wall,
+    dense,
+    mixed,
+    attended,
+    resid,
+    both,
+    aux,
+    rows_s,
+    lse,
+    sums,
+    dprobs_s,
+    stage,
+    win,
+    wout,
+    given,
+    upstream_s,
+    gate_s,
+    dres_s,
+    dattended,
+    acc_k,
+    acc_v,
+    dq_t,
+    gd,
+    gsums,
+    gs,
+    rc,
+    s1,
+    rxa,
+    ryb,
+    s2a,
+    s2b,
+    rya,
+    rxb,
+    s3,
+    rz,
+    fb,
+    dz,
+    dx,
+    zs,
+    zr,
+    hop_s,
+    hop_r,
+    local,
+    outward,
+    send,
+    land,
+):
+    att_t = gd.at[:, pl.ds(DENSE_COLS - GRID, GRID)]
+    held = gd.at[:, pl.ds(0, FCH)]
+    db = stage.at[1]
+    p = Place()
+    peers = [p.core_peer(), p.x_peer(), p.y_peer()] + [p.z_peer(k) for k in range(1, ZS)]
+    barrier = pltpu.get_barrier_semaphore()
+    for peer in peers:
+        pl.semaphore_signal(barrier, inc=1, device_id=peer, device_id_type=MESH)
+    pl.semaphore_wait(barrier, len(peers))
+    gather = Gather(
+        p,
+        mine,
+        wall,
+        zs,
+        zr,
+        hop_s.at[0],
+        hop_r.at[0],
+        hop_s.at[1],
+        hop_r.at[1],
+        hop_s.at[2],
+        hop_r.at[2],
+        hop_s.at[3],
+        hop_r.at[3],
+    )
+    scatter = Scatter(p, gs, rc, s1, rxa, ryb, s2a, s2b, rya, rxb, s3, rz, fb, send, land)
+
+    def dz_copy(k):
+        return remote(dmine, db.at[p.x, p.c, p.z, :, :, pl.ds(0, DENSE_LANES)], (dz.at[0, k], dz.at[1, k]), p.z_peer(k))
+
+    def dz_landed(k):
+        here = db.at[p.x, p.c, p.z_behind(k), :, :, pl.ds(0, DENSE_LANES)]
+        return remote(here, here, (dz.at[0, k], dz.at[1, k]), p.z_peer(k))
+
+    def dx_copy(x):
+        here = db.at[x, p.c, :, :, :, pl.ds(0, DENSE_LANES)]
+        return remote(here, here, (dx.at[0, 0], dx.at[1, 0]), p.x_peer())
+
+    def da_copy(x, c):
+        here = db.at[x, c, :, :, :, pl.ds(0, DENSE_LANES)]
+        return remote(here, here, (dx.at[0, 1], dx.at[1, 1]), p.core_peer())
+
+    def db_copy(x, c):
+        here = db.at[x, c, :, :, :, pl.ds(0, DENSE_LANES)]
+        return remote(here, here, (dx.at[0, 2], dx.at[1, 2]), p.core_peer())
+
+    cot_copy = pltpu.make_async_copy(cot_ref, both.at[:, pl.ds(D, D)], local.at[3])
+    cot_copy.start()
+    for k in range(1, ZS):
+        dz_copy(k).start()
+    own_copy = pltpu.make_async_copy(mine, wall.at[:, p.x, p.c, p.z], local.at[2])
+    own_copy.start()
+    gather.t0(0)
+    gather.t0(1)
+    db[p.x, p.c, p.z, :, :, pl.ds(0, DENSE_LANES)] = dmine[...]
+
+    def route_step(image, carry):
+        task = task_ref[image]
+        routing(task, count_ref[task], ids_ref, valid_ref, image, rows_s)
+        return carry
+
+    lax.fori_loop(0, images, route_step, 0)
+    for k in range(1, ZS):
+        dz_landed(k).wait_recv()
+    dx_copy(p.x).start()
+    da_copy(p.x, p.c).start()
+    dx_copy(1 - p.x).wait_recv()
+    db_copy(1 - p.x, p.c).start()
+    da_copy(p.x, 1 - p.c).wait_recv()
+    db_copy(1 - p.x, 1 - p.c).wait_recv()
+    own_copy.wait()
+    cot_copy.wait()
+    for k in range(1, ZS):
+        dz_copy(k).wait_send()
+    dx_copy(p.x).wait_send()
+    da_copy(p.x, p.c).wait_send()
+    db_copy(1 - p.x, p.c).wait_send()
+    for z in range(ZS):
+        for x in range(XS):
+            rows = pl.ds((z * XS + x) * HALF_ROWS, HALF_ROWS)
+            for half in range(2):
+                one = db[x, 0, z, half, :, pl.ds(0, DENSE_LANES)].astype(F32)
+                two = db[x, 1, z, half, :, pl.ds(0, DENSE_LANES)].astype(F32)
+                for part in range(2):
+                    cut = slice(part * 24, part * 24 + 24)
+                    at = half * 1024 + part * DENSE_LANES
+                    width = min(DENSE_LANES, MISC + 128 - at)
+                    if width > 0:
+                        dense[rows, at : at + width] = jnp.concatenate(
+                            [one[cut, :width], two[cut, :width]], axis=0
+                        ).astype(BF16)
+
+    misc = dense[:, MISC:].astype(F32).T
+    lane = lanes((GRID, 128))
+
+    def forward_ticks(step, point):
+        def when(at, action):
+            @pl.when(step == at)
+            def _():
+                action()
+
+        def first(e):
+            gather.t1(e)
+            gather.t0(e + 2)
+
+        def load(e):
+            gather.t4(e)
+            pltpu.make_async_copy(wall.at[e], stage.at[e], local.at[e]).start()
+
+        if point == 0:
+            when(0, lambda: first(0))
+            when(1, lambda: gather.t2(0))
+            when(2, lambda: gather.t3(0))
+            when(3, lambda: first(2))
+            when(4, lambda: gather.t2(2))
+        else:
+            when(1, lambda: first(1))
+            when(2, lambda: gather.t2(1))
+            when(3, lambda: (gather.t3(1), load(0)))
+
+    def forward_image(image, carry):
+        at_row = pl.multiple_of(image * GRID, GRID)
+        mine_rows = pl.ds(at_row, GRID)
+        task = task_ref[image]
+        inputs = tokens_ref[mine_rows, :].astype(F32)
+        unit_a, _ = norm_rows(inputs)
+        normed_a = (unit_a * misc[0:1] + misc[1:2]).astype(BF16)
+        mixed[mine_rows, :] = nn(normed_a, dense[:, : 3 * D]).astype(BF16)
+        live_col = column_of(valid_ref[pl.ds(image, 1), :].astype(F32))
+        key_ext = jnp.where((lane == 0) & (live_col < 0.5), NEGATIVE, 0.0).astype(BF16)
+        query_ext = jnp.where(lanes((QB, 128)) == 0, 1.0, 0.0).astype(BF16)
+        ones_rows = jnp.ones((16, GRID), BF16)
+        half = lanes((QB, 128)) // HEAD_DIM
+
+        def pair_step(pair, carry):
+            at = pl.multiple_of(pair * 128, 128)
+            keys = mixed[mine_rows, pl.ds(D + at, 128)]
+            values = mixed[mine_rows, pl.ds(2 * D + at, 128)]
+            key_full = jnp.concatenate([keys, key_ext], axis=1)
+            value_t = jnp.concatenate([values.astype(F32).T.astype(BF16), ones_rows], axis=0)
+            for block in range(GRID // QB):
+                span = pl.ds(block * QB, QB)
+                query = mixed[pl.ds(pl.multiple_of(at_row + block * QB, QB), QB), pl.ds(at, 128)].astype(F32) * SCALE
+                for part in range(2):
+                    own = jnp.where(half == part, query, 0.0).astype(BF16)
+                    scores = nt(key_full, jnp.concatenate([own, query_ext], axis=1))
+                    top = jnp.max(scores, axis=0, keepdims=True)
+                    raised = jnp.exp(scores - top).astype(BF16)
+                    produced = nn(value_t, raised)
+                    total = produced[128:129]
+                    mine_part = produced[part * HEAD_DIM : (part + 1) * HEAD_DIM] / total
+                    att_t[pl.ds(at + part * HEAD_DIM, HEAD_DIM), span] = mine_part
+                    lse[image, pl.ds(pair * 2 + part, 1), span] = top + jnp.log(total)
+                if block % 2 == 1:
+                    forward_ticks(image * PAIRS + pair, block // 2)
+            return carry
+
+        lax.fori_loop(0, PAIRS, pair_step, 0)
+        seen = att_t[...].T.astype(BF16)
+        attended[mine_rows, :] = seen
+        branch = inputs + nn(seen, dense[:, 3 * D : MISC])
+        resid[mine_rows, :] = branch
+        unit_b, _ = norm_rows(branch)
+        normed_b = (unit_b * misc[2:3] + misc[3:4]).astype(BF16)
+        both[mine_rows, :D] = normed_b
+        logits = nn(normed_b, router_of(dense, task))
+        logits = jnp.where(lane < EXPERTS, logits, NEGATIVE)
+        raised = jnp.exp(logits - jnp.max(logits, axis=-1, keepdims=True))
+        probs = raised / jnp.sum(raised, axis=-1, keepdims=True)
+        aux[mine_rows, :] = probs
+        probs_t = probs.T[:EXPERTS]
+        rows_s[image, EXPERTS:] = jnp.where(rows_s[image, :EXPERTS] >= 0.0, probs_t, 0.0)
+        return carry
+
+    lax.fori_loop(0, images, forward_image, 0)
+
+    def finish(e, halves):
+        first, second = halves
+        grad_in_ref[e, :, :WIDE_LANES] = first[:24]
+        grad_in_ref[e, :, WIDE_LANES:] = first[24:]
+        grad_out_ref[e, :HALF_ROWS] = second[:, :D]
+        grad_out_ref[e, HALF_ROWS:] = second[:, D:]
+
+    def guard(e, action):
+        @pl.when((e >= 0) & (e < EXPERTS))
+        def _():
+            action(e)
+
+    def point_a(i):
+        guard(i - 4, lambda e: scatter.r4(lax.rem(e, 2)))
+        guard(i - 3, lambda e: scatter.r3(lax.rem(e, 2)))
+
+    def point_b(i):
+        guard(i - 2, lambda e: scatter.r2(lax.rem(e, 2)))
+        guard(i - 1, lambda e: scatter.r1(lax.rem(e, 2)))
+        guard(i - 4, lambda e: finish(e, scatter.r5(lax.rem(e, 2))))
+
+    slot_at = lax.broadcasted_iota(jnp.int32, (CAP, GRID), 0).astype(F32)
+    c1 = math.sqrt(2.0 / math.pi)
+    c3 = c1 * 0.044715
+
+    def expert_step(expert, carry):
+        slot = lax.rem(expert, 2)
+
+        @pl.when(expert + 3 < EXPERTS)
+        def _():
+            gather.t1(expert + 3)
+
+        @pl.when(expert + 5 < EXPERTS)
+        def _():
+            gather.t0(expert + 5)
+
+        point_a(expert)
+        pltpu.make_async_copy(wall.at[expert], stage.at[slot], local.at[slot]).wait()
+        for z in range(ZS):
+            for x in range(XS):
+                chip = z * XS + x
+                one = stage[slot, x, 0, z, 0].astype(F32)
+                two = stage[slot, x, 1, z, 0].astype(F32)
+                rows = pl.ds(chip * HALF_ROWS, HALF_ROWS)
+                win[rows, :WIDE_LANES] = jnp.concatenate([one[:24], two[:24]], axis=0).astype(BF16)
+                win[rows, WIDE_LANES:] = jnp.concatenate([one[24:], two[24:]], axis=0).astype(BF16)
+                for c in range(CORES):
+                    base = (chip * CORES + c) * 96
+                    wout[pl.ds(base, HALF_ROWS), :] = stage[slot, x, c, z, 1, :, :D]
+                    wout[pl.ds(base + HALF_ROWS, HALF_ROWS), :] = stage[slot, x, c, z, 1, :, D:]
+        for image in range(images):
+            part = pl.ds(image * CAP, CAP)
+            slot_row = rows_s[image, pl.ds(expert, 1), :]
+            gate_row = rows_s[image, pl.ds(EXPERTS + expert, 1), :]
+            match = slot_at == slot_row
+            sent = nn(jnp.where(match, 1.0, 0.0).astype(BF16), both[pl.ds(image * GRID, GRID), :])
+            gate = jnp.sum(jnp.where(match, gate_row, 0.0), axis=1, keepdims=True)
+            given[part, :] = sent[:, :D].astype(BF16)
+            upstream_s[part, :] = sent[:, D:].astype(BF16)
+            gate_s[part, :] = jnp.broadcast_to(gate, (CAP, 128))
+            dres_s[part, :] = (gate * sent[:, D:]).astype(BF16)
+        slots = given[...]
+        dres = dres_s[...]
+        result = jnp.zeros((images * CAP, D), F32)
+        back = jnp.zeros((images * CAP, D), F32)
+        for chunk in range(FF // FCH):
+            span = pl.ds(chunk * FCH, FCH)
+            w_in = win[:, span]
+            w_out = wout[span, :]
+            pre = nn(slots, w_in)
+            square = pre * pre
+            curve = jnp.tanh(pre * (c1 + c3 * square))
+            lifted = 0.5 * (1.0 + curve)
+            hidden = (pre * lifted).astype(BF16)
+            slope = lifted + (0.5 * pre) * (1.0 - curve * curve) * (c1 + (3.0 * c3) * square)
+            result = result + nn(hidden, w_out)
+            dpre = (nt(dres, w_out) * slope).astype(BF16)
+            back = back + nt(dpre, w_in)
+            term = tn(hidden, dres)
+            for one in range(FCH // 96):
+                w = chunk * (FCH // 96) + one
+                z, x, c = w // (XS * CORES), (w // CORES) % XS, w % CORES
+                gs[slot, c, x, z, 1, :, :D] = term[one * 96 : one * 96 + 48].astype(BF16)
+                gs[slot, c, x, z, 1, :, D:] = term[one * 96 + 48 : one * 96 + 96].astype(BF16)
+            term = tn(slots, dpre)
+            if chunk == 0:
+                held[...] = term
+                guard(expert + 2, gather_third)
+                guard(expert + 1, load_next)
+                point_b(expert)
+            else:
+                for w in range(ZS * XS * CORES):
+                    z, x, c = w // (XS * CORES), (w // CORES) % XS, w % CORES
+                    rows = slice(w * 24, w * 24 + 24)
+                    gs[slot, c, x, z, 0] = jnp.concatenate([held[rows, :], term[rows]], axis=0).astype(BF16)
+        result = result.astype(BF16).astype(F32)
+        dgate = jnp.sum(result * upstream_s[...].astype(F32), axis=1, keepdims=True)
+        gated = result * gate_s[:, :1]
+        returned = jnp.concatenate([gated.astype(BF16), back.astype(BF16)], axis=1)
+        scatter.r0(slot)
+
+        @pl.when(expert + 3 < EXPERTS)
+        def _():
+            gather.t2(expert + 3)
+
+        for image in range(images):
+            part = slice(image * CAP, (image + 1) * CAP)
+            span = pl.ds(image * GRID, GRID)
+            slot_row = rows_s[image, pl.ds(expert, 1), :]
+            match = slot_at == slot_row
+            dprobs_s[image, pl.ds(expert, 1), :] = jnp.sum(
+                jnp.where(match, dgate[part], 0.0), axis=0, keepdims=True
+            )
+            hit = jnp.where(match, 1.0, 0.0).astype(BF16)
+            landed = tn(hit, returned[part])
+            sums[span, :] = jnp.where(expert == 0, landed, sums[span, :] + landed)
+        return carry
+
+    def gather_third(e):
+        gather.t3(e)
+
+    def load_next(e):
+        gather.t4(e)
+        slot = lax.rem(e, 2)
+        pltpu.make_async_copy(wall.at[e], stage.at[slot], local.at[slot]).start()
+
+    lax.fori_loop(0, EXPERTS, expert_step, 0)
+
+    def out_copy(image):
+        rows = pl.ds(pl.multiple_of(image * GRID, GRID), GRID)
+        return pltpu.make_async_copy(both.at[rows, pl.ds(D, D)], output_ref.at[rows, :], outward.at[0, image])
+
+    def grad_copy(image):
+        rows = pl.ds(pl.multiple_of(image * GRID, GRID), GRID)
+        return pltpu.make_async_copy(both.at[rows, pl.ds(0, D)], grad_tokens_ref.at[rows, :], outward.at[1, image])
+
+    small = lanes((QB, 128))
+    half = small // HEAD_DIM
+
+    def backward_image(image, carry):
+        at_row = pl.multiple_of(image * GRID, GRID)
+        mine_rows = pl.ds(at_row, GRID)
+        task = task_ref[image]
+        upstream = both[mine_rows, D:].astype(F32)
+        branch = resid[mine_rows, :]
+        unit_b, inverse_b = norm_rows(branch)
+        probs = aux[mine_rows, :]
+        dprobs = jnp.concatenate([dprobs_s[image], jnp.zeros((128 - EXPERTS, GRID), F32)], axis=0).T
+        dlogits = probs * (dprobs - jnp.sum(dprobs * probs, axis=-1, keepdims=True))
+        dlogits = dlogits.astype(BF16)
+        grad_router = tn(both[mine_rows, :D], dlogits)
+        both[mine_rows, D:] = (branch + sums[mine_rows, :D]).astype(BF16)
+        out_copy(image).start()
+        dnormed_b = sums[mine_rows, D:] + nt(dlogits, router_of(dense, task))
+        dresid = upstream + norm_back(dnormed_b, unit_b, inverse_b, misc[2:3])
+        resid[mine_rows, :] = dresid
+        dbranch = dresid.astype(BF16)
+        grad_proj_out = tn(attended[mine_rows, :], dbranch)
+        dattended[...] = nt(dbranch, dense[:, 3 * D : MISC]).astype(BF16)
+        moe_sums = jnp.concatenate(
+            [jnp.sum(dnormed_b * unit_b, axis=0, keepdims=True), jnp.sum(dnormed_b, axis=0, keepdims=True)], axis=0
+        )
+        live_col = column_of(valid_ref[pl.ds(image, 1), :].astype(F32))
+        lse_col = jnp.concatenate([lse[image], jnp.zeros((120, GRID), F32)], axis=0).T
+        key_ext = jnp.where((lane == 0) & (live_col < 0.5), NEGATIVE, 0.0)
+        key_ext = jnp.where((lane >= 1) & (lane <= 3), 1.0, key_ext).astype(BF16)
+        value_ext = jnp.where(lane < 3, 1.0, 0.0).astype(BF16)
+
+        def pair_step(pair, carry):
+            step = EXPERTS + image * PAIRS + pair
+            point_a(step)
+            at = pl.multiple_of(pair * 128, 128)
+            keys = mixed[mine_rows, pl.ds(D + at, 128)]
+            values = mixed[mine_rows, pl.ds(2 * D + at, 128)]
+            key_full = jnp.concatenate([keys, key_ext], axis=1)
+            value_full = jnp.concatenate([values, value_ext], axis=1)
+            key_t = keys.astype(F32).T.astype(BF16)
+            for block in range(GRID // QB):
+                span = pl.ds(block * QB, QB)
+                rows_here = pl.ds(pl.multiple_of(at_row + block * QB, QB), QB)
+                query = mixed[rows_here, pl.ds(at, 128)].astype(F32) * SCALE
+                grad = dattended[span, pl.ds(at, 128)].astype(F32)
+                seen = attended[rows_here, pl.ds(at, 128)].astype(F32) * grad
+                for part in range(2):
+                    own = half == part
+                    inner = jnp.sum(jnp.where(own, seen, 0.0), axis=-1, keepdims=True)
+                    high, mid, low = split3(-inner)
+                    grad_ext = jnp.where(
+                        small == 0, high, jnp.where(small == 1, mid, jnp.where(small == 2, low, 0.0))
+                    ).astype(BF16)
+                    head = pair * 2 + part
+                    shift = jnp.sum(
+                        jnp.where(small == head, lse_col[block * QB : (block + 1) * QB], 0.0),
+                        axis=-1,
+                        keepdims=True,
+                    )
+                    high, mid, low = split3(-shift)
+                    query_ext = jnp.where(
+                        small == 0,
+                        1.0,
+                        jnp.where(
+                            small == 1, high, jnp.where(small == 2, mid, jnp.where(small == 3, low, 0.0))
+                        ),
+                    ).astype(BF16)
+                    my_query = jnp.where(own, query, 0.0).astype(BF16)
+                    my_grad = jnp.where(own, grad, 0.0).astype(BF16)
+                    weights = jnp.exp(nt(key_full, jnp.concatenate([my_query, query_ext], axis=1)))
+                    drift = nt(value_full, jnp.concatenate([my_grad, grad_ext], axis=1))
+                    dscores = (weights * drift).astype(BF16)
+                    dkey = nn(dscores, my_query)
+                    dvalue = nn(weights.astype(BF16), my_grad)
+                    if block == 0 and part == 0:
+                        acc_k[...] = dkey
+                        acc_v[...] = dvalue
+                    else:
+                        acc_k[...] += dkey
+                        acc_v[...] += dvalue
+                    rows = slice(part * HEAD_DIM, (part + 1) * HEAD_DIM)
+                    dq_t[rows, span] = nn(key_t[rows], dscores)
+                if block == 1:
+                    point_b(step)
+            mixed[mine_rows, pl.ds(at, 128)] = (dq_t[...].T * SCALE).astype(BF16)
+            mixed[mine_rows, pl.ds(D + at, 128)] = acc_k[...].astype(BF16)
+            mixed[mine_rows, pl.ds(2 * D + at, 128)] = acc_v[...].astype(BF16)
+            return carry
+
+        lax.fori_loop(0, PAIRS, pair_step, 0)
+        unit_a, inverse_a = norm_rows(tokens_ref[mine_rows, :].astype(F32))
+        normed_a = (unit_a * misc[0:1] + misc[1:2]).astype(BF16)
+        dmixed = mixed[mine_rows, :]
+        grad_proj_in = tn(normed_a, dmixed)
+        dnormed_a = nt(dmixed, dense[:, : 3 * D])
+        both[mine_rows, :D] = (
+            resid[mine_rows, :] + norm_back(dnormed_a, unit_a, inverse_a, misc[0:1])
+        ).astype(BF16)
+        grad_copy(image).start()
+        totals = jnp.concatenate(
+            [
+                jnp.sum(dnormed_a * unit_a, axis=0, keepdims=True),
+                jnp.sum(dnormed_a, axis=0, keepdims=True),
+                moe_sums,
+                jnp.zeros((4, D), F32),
+            ],
+            axis=0,
+        )
+        placed = jnp.where(task == 0, pltpu.roll(grad_router, 4, 1), pltpu.roll(grad_router, 12, 1))
+        fresh = image == 0
+        gd[:, : 3 * D] = jnp.where(fresh, grad_proj_in, gd[:, : 3 * D] + grad_proj_in)
+        gd[:, 3 * D : MISC] = jnp.where(fresh, grad_proj_out, gd[:, 3 * D : MISC] + grad_proj_out)
+        gd[:, MISC : MISC + 128] = jnp.where(fresh, placed, gd[:, MISC : MISC + 128] + placed)
+        gsums[...] = jnp.where(fresh, totals, gsums[...] + totals)
+        return carry
+
+    gd[...] = jnp.zeros_like(gd)
+    gsums[...] = jnp.zeros_like(gsums)
+    lax.fori_loop(0, images, backward_image, 0)
+
+    columns = jnp.concatenate([gsums[...], jnp.zeros((120, D), F32)], axis=0).T
+    gd[:, MISC : MISC + 128] = jnp.where(lanes((D, 128)) < 4, columns, gd[:, MISC : MISC + 128])
+    for w in range(ZS * XS * CORES):
+        z, x, c = w // (XS * CORES), (w // CORES) % XS, w % CORES
+        rows = slice(w * 24, w * 24 + 24)
+        for part in range(2):
+            at = part * 1024
+            gs[0, c, x, z, part, :, :DENSE_LANES] = jnp.concatenate(
+                [gd[rows, at : at + DENSE_LANES], gd[rows, at + DENSE_LANES : at + 2 * DENSE_LANES]], axis=0
+            ).astype(BF16)
+    scatter.r0(0, DENSE_LANES)
+    scatter.r1(0, DENSE_LANES)
+    scatter.r2(0, DENSE_LANES)
+    scatter.r3(0, DENSE_LANES)
+    scatter.r4(0, DENSE_LANES)
+    for part, value in enumerate(scatter.r5(0, DENSE_LANES)):
+        at = part * 1024
+        grad_dense_ref[:, at : at + DENSE_LANES] = value[:24]
+        grad_dense_ref[:, at + DENSE_LANES : at + 2 * DENSE_LANES] = value[24:]
+
+    def drain(e, carry):
+        gather.drain(e)
+        return carry
+
+    lax.fori_loop(0, EXPERTS, drain, 0)
+
+    def written(image, carry):
+        out_copy(image).wait()
+        grad_copy(image).wait()
+        return carry
+
+    lax.fori_loop(0, images, written, 0)
+
+
+def whole_call(task_ids, top_counts, tokens, cotangent, valid, ids_t, dmine, mine):
+    images = valid.shape[0]
+    rows = images * GRID
+    smem = pl.BlockSpec(memory_space=pltpu.SMEM)
+    vmem = pl.BlockSpec(memory_space=pltpu.VMEM)
+    anywhere = pl.BlockSpec(memory_space=pl.ANY)
+    piece = (HALF_ROWS, WIDE_LANES)
+    sem = pltpu.SemaphoreType.DMA
+    return pl.pallas_call(
+        functools.partial(whole_kernel, images),
+        in_specs=[smem, smem, vmem, anywhere, vmem, vmem, vmem, anywhere],
+        out_specs=[anywhere, anywhere, vmem, vmem, vmem, anywhere],
+        out_shape=[
+            jax.ShapeDtypeStruct((rows, D), BF16),
+            jax.ShapeDtypeStruct((rows, D), BF16),
+            jax.ShapeDtypeStruct((EXPERTS, 24, FF), F32),
+            jax.ShapeDtypeStruct((EXPERTS, 96, D), F32),
+            jax.ShapeDtypeStruct((24, DENSE_COLS), F32),
+            jax.ShapeDtypeStruct((EXPERTS, XS, CORES, ZS, 2) + piece, BF16),
+        ],
+        scratch_shapes=[
+            pltpu.VMEM((D, DENSE), BF16),
+            pltpu.VMEM((rows, 3 * D), BF16),
+            pltpu.VMEM((rows, D), BF16),
+            pltpu.VMEM((rows, D), F32),
+            pltpu.VMEM((rows, 2 * D), BF16),
+            pltpu.VMEM((rows, 128), F32),
+            pltpu.VMEM((images, 2 * EXPERTS, GRID), F32),
+            pltpu.VMEM((images, 8, GRID), F32),
+            pltpu.VMEM((rows, 2 * D), F32),
+            pltpu.VMEM((images, EXPERTS, GRID), F32),
+            pltpu.VMEM((2, XS, CORES, ZS, 2) + piece, BF16),
+            pltpu.VMEM((D, FF), BF16),
+            pltpu.VMEM((FF, D), BF16),
+            pltpu.VMEM((images * CAP, D), BF16),
+            pltpu.VMEM((images * CAP, D), BF16),
+            pltpu.VMEM((images * CAP, 128), F32),
+            pltpu.VMEM((images * CAP, D), BF16),
+            pltpu.VMEM((GRID, D), BF16),
+            pltpu.VMEM((GRID, 128), F32),
+            pltpu.VMEM((GRID, 128), F32),
+            pltpu.VMEM((128, GRID), F32),
+            pltpu.VMEM((D, DENSE_COLS), F32),
+            pltpu.VMEM((8, D), F32),
+            pltpu.VMEM((2, CORES, XS, ZS, 2) + piece, BF16),
+            pltpu.VMEM((2, XS, ZS, 2) + piece, BF16),
+            pltpu.VMEM((XS, ZS, 2) + piece, BF16),
+            pltpu.VMEM((2, 2, 2) + piece, BF16),
+            pltpu.VMEM((2, XS, 2) + piece, BF16),
+            pltpu.VMEM((2, 2) + piece, BF16),
+            pltpu.VMEM((XS, 2) + piece, BF16),
+            pltpu.VMEM((2, 2) + piece, BF16),
+            pltpu.VMEM((2, 2) + piece, BF16),
+            pltpu.VMEM((ZS,) + piece, BF16),
+            pltpu.VMEM((2, ZS - 1) + piece, BF16),
+            pltpu.VMEM((2, 2) + piece, BF16),
+            sem((2, ZS)),
+            sem((2, 3)),
+            sem((EXPERTS, ZS - 1)),
+            sem((EXPERTS, ZS - 1)),
+            sem((4, EXPERTS)),
+            sem((4, EXPERTS)),
+            sem((4,)),
+            sem((2, images)),
+            sem((9, 2)),
+            sem((9, 2)),
+        ],
+        compiler_params=pltpu.CompilerParams(
+            vmem_limit_bytes=VMEM_LIMIT, collective_id=0, has_side_effects=True
+        ),
+        name="whole_step",
+    )(task_ids, top_counts, tokens, cotangent, valid, ids_t, dmine, mine)
+
+
+def whole_body(
+    tokens,
+    cotangent,
+    valid,
+    task_ids,
+    top_counts,
+    expert_ids,
+    attn_gain,
+    attn_shift,
+    proj_in,
+    proj_out,
+    moe_gain,
+    moe_shift,
+    router,
+    expert_in,
+    expert_out,
+):
+    own = attn_gain.shape[0]
+    vectors = jnp.stack([attn_gain, attn_shift, moe_gain, moe_shift], axis=1)
+    blank = jnp.zeros((own, DENSE_COLS - MISC - 4 - TASKS * EXPERTS), BF16)
+    packed = jnp.concatenate([proj_in, proj_out, vectors, router[0], router[1], blank], axis=1)
+    dmine = packed.reshape(own, 2, 2, DENSE_LANES).transpose(1, 2, 0, 3).reshape(2, HALF_ROWS, DENSE_LANES)
+    first = expert_in.reshape(EXPERTS, own, 2, WIDE_LANES).transpose(0, 2, 1, 3).reshape(EXPERTS, HALF_ROWS, WIDE_LANES)
+    second = jnp.concatenate([expert_out[:, :HALF_ROWS], expert_out[:, HALF_ROWS:]], axis=2)
+    mine = jnp.stack([first, second], axis=1)
+    output, grad_tokens, grad_in, grad_out, grad_dense, _ = whole_call(
+        task_ids, top_counts, tokens, cotangent, valid, expert_ids.T, dmine, mine
+    )
+    columns = grad_dense[:, MISC : MISC + 4].T
+    grad_router = jnp.stack(
+        [grad_dense[:, MISC + 4 : MISC + 12], grad_dense[:, MISC + 12 : MISC + 20]], axis=0
+    )
+    return (
+        output,
+        grad_tokens,
+        columns[0],
+        columns[1],
+        grad_dense[:, : 3 * D],
+        grad_dense[:, 3 * D : MISC],
+        columns[2],
+        columns[3],
+        grad_router,
+        grad_in,
+        grad_out,
+    )
 
 
 def body(
@@ -599,8 +1511,9 @@
 def solution(mesh):
     rows = P(("narrow", "wide"), None)
     middle = P(None, "wide", None)
+    one_kernel = mesh.shape["narrow"] == 2 and mesh.shape["wide"] == ZS * XS * CORES
     return jax.shard_map(
-        body,
+        whole_body if one_kernel else body,
         mesh=mesh,
         in_specs=(
             rows,

time: 653 us -> 301 us (0.46)
  waiting for transfers between devices: 426 us -> 0 us
  Pallas kernels: 182 us -> 278 us
  between operations: 14.2 us -> 0.71 us
    all_gather x3 -> x0, waiting for transfers between devices: 153 us -> none  [the longest x1 81.9 us: body(): full_out = lax.all_gather(expert_out, 'wide', axis=1, tiled=True)]
    reduce_scatter x1 -> x0, waiting for transfers between devices: 115 us -> none  [body(): lax.psum_scatter(grad_out, 'wide', scatter_dimension=1, tiled=True)]
    unnamed x9 -> x0, waiting for transfers between devices: 110 us -> none
    pallas_call x3 -> x1, Pallas kernels: 182 us -> 278 us  [whole_call(): pl.pallas_call(functools.partial(whole_kernel, images), in_specs=[smem, s...]
    psum x1 -> x0, waiting for transfers between devices: 47.8 us -> none  [body(): lax.psum((part_in, part_out, part_dense), 'narrow')]
    convert_element_type x4 -> x0, other arithmetic: 7.17 us -> none  [the longest x1 2.96 us: body(): grad_dense.astype(BF16)]
    unnamed x8 -> x12, local copies, waits for them, and re-layouts: 13.2 us -> 7.38 us
  transfers between devices with their start and end apart: 7 -> 0, of which waited for: 7 -> 0; matrix products, arithmetic and copies ran while one was open for 1% -> 0% of each run, Pallas kernels for 16% -> 0%
where the time goes in v3:
time: 301 us; the launch traced here: 300 us
  Pallas kernels  278 us (92%)
  local copies, waits for them, and re-layouts  19.5 us (6%)
    pallas_call x1, Pallas kernels, whole_call(): pl.pallas_call(functools.partial(whole_kernel, images), in_specs=[smem, s...  278 us
    unnamed x12, local copies, waits for them, and re-layouts  7.38 us

profile of v3, /device:TPU:0, one launch (start us, length us, event | category | flops | bytes accessed | tf_op | source)
XLA Modules:
  0.0 300.1 jit_solution(2855297255807883710)
XLA Ops:
  0.6 0.0 copy-start.3
  0.7 0.8 slice_bitcast_fusion.3
  1.4 0.1 copy.49
  1.5 0.1 copy.48
  1.6 0.7 copy.44
  2.3 0.7 copy.45
  3.1 0.7 copy.46
  3.8 0.7 copy.47
  4.6 0.9 concatenate.6
  5.6 0.7 copy.50
  6.2 1.1 copy.56
  7.3 0.0 copy-done.3
  7.3 0.1 fusion
  7.4 0.1 maximum_bitcast_fusion
  7.5 1.1 pad_maximum_fusion.mine
  8.6 278.2 %whole_step.1 = (bf16[2048,384]{1,0:T(8,128)(2,1)}, bf16[2048,384]{1,0:T(8,128)(2,1)}, f32[8,24,1536]{2,1,0:T(8,128)}, f32[8,96,384]{2,1,0:T(8,128)}, f32[24,204...) custom-call(s32[2]{0:T(128)} %task_ref.1, s32[2]{0:T(128)} %count_ref.1, bf16[2048,384]{1,0:T(8,128)(2,1)} %tokens_ref.1, ...), custom_call_target="tpu_custom_call" | custom-call | tf_op jit(solution)/shard_map/whole_step/pallas_call | solution.py:1334
  286.8 0.7 slice_bitcast_fusion.2
  287.5 0.7 slice_reduce_fusion
  288.2 0.9 slice_bitcast_fusion.1
  289.1 0.1 copy.52
  289.1 0.1 copy.53
  289.2 0.6 pad_maximum_fusion.1
  289.8 1.4 slice.47
  291.2 1.5 slice.46
  292.8 0.0 copy-start
  292.8 2.8 copy.61
  295.6 0.0 copy-done
  295.6 0.0 copy-start.2
  295.6 1.1 copy.62
  296.7 0.7 copy-done.2
  297.4 0.0 copy-start.1
  297.4 1.0 copy.63
  298.4 0.7 copy-done.1
  299.1 1.0 copy.64
  (2 shorter events, 0.1 us)
Async XLA Ops:
  0.6 6.7 %copy-start.3 = (bf16[8,96,384]{2,1,0:T(8,128)(2,1)S(1)}, bf16[8,96,384]{2,1,0:T(8,128)(2,1)}, u32[]{:S(2)}) copy-start(bf16[8,96,384]{2,1,0:T(8,128)(2,1)} %param.29) | copy-start | bytes 1769476
  292.8 2.8 copy-start
  295.6 1.8 copy-start.2
  297.4 1.7 copy-start.1
